TPU v7x, 128 devices: a whole 4x4x4 slice. The times are simulated.
128 devices in a mesh: ctx: 16 (over y, x_hi, core), tp: 8 (over x_lo, z).
Axes of the slice: x: 4 (x_hi: 2, x_lo: 2; x = x_hi * 2 + x_lo), y: 4, z: 4, core: 2. Of those that a mesh axis runs over, the one named last changes fastest.
Arguments:
- inputs: bfloat16 [2048, 4096], P('ctx', 'tp'), may hold values from -6 to 6
- residue: float32 [4096, 16], P('tp'), may hold values from -1.5 to 1.5
- log_rate: float32 [4096, 16], P('tp'), may hold values from -1 to 6.5
- skip: float32 [4096], P('tp'), may hold values from 0.5 to 1.5
- out_weight: bfloat16 [4096, 8192], P('tp'), may hold values from -0.09375 to 0.09375
- out_grad: bfloat16 [2048, 8192], P(('ctx', 'tp')), may hold values from -6 to 6
Outputs:
- out: bfloat16 [2048, 8192], P(('ctx', 'tp'))
- grad_input: bfloat16 [2048, 4096], P('ctx', 'tp')
- grad_residue: float32 [4096, 16], P('tp')
- grad_log_rate: float32 [4096, 16], P('tp')
- grad_skip: float32 [4096], P('tp')
All inputs are finite; a program needn't handle non-finite values.
Results may differ from a plain program's by a relative error of at most 0.02.
Values may be sent and summed in bfloat16 or wider, within the bound.
A program may use at most 128 MiB of HBM per device.

v0:
```python
import functools
import math

import jax
import jax.numpy as jnp
from jax import lax
from jax.experimental import pallas as pl
from jax.experimental.pallas import tpu as pltpu
from jax.sharding import PartitionSpec as P

MESH = pl.DeviceIdType.MESH
F32 = jnp.float32
BF16 = jnp.bfloat16
SUB = 8
LANE = 128
NX, NZ = 2, 4


def kernel(
    seq,
    n_ctx,
    x_ref,
    res_ref,
    lr_ref,
    skip_ref,
    w_hbm,
    og_hbm,
    out_ref,
    gi_ref,
    gres_ref,
    glog_ref,
    gskip_ref,
    w_v,
    og,
    part,
    hall,
    x32,
    y32,
    g32,
    gacc,
    mb,
    rate_t,
    c_t,
    rate8,
    a8,
    c8,
    ex8,
    in8,
    st_t,
    s_send,
    s_recv,
    r_send,
    r_recv,
    g8,
    m8,
    k8,
    red,
    rr,
    fin,
    bx1,
    bl1,
    br1,
    bl2,
    br2,
    bx3,
    al1,
    ar1,
    al2,
    ar2,
    w_sem,
    own_sem,
    ag_s,
    ag_r,
    rs_s,
    rs_r,
    s_ss,
    s_rs,
    r_ss,
    r_rs,
    p_ss,
    p_rs,
    q_ss,
    q_rs,
):
    tok, chans = x_ref.shape
    modes = res_ref.shape[1]
    dim = w_v.shape[1]
    rows = tok // (NX * NZ)
    steps = tok // SUB
    lanes = chans // LANE
    half, quarter = dim // 2, dim // 4
    col_block = min(1024, half)
    n_blocks = dim // col_block

    me = lax.axis_index("ctx")
    tp = lax.axis_index("tp")
    xl, z = tp // NZ, lax.rem(tp, NZ)
    ox = 1 - xl
    zr, zl, zo = lax.rem(z + 1, NZ), lax.rem(z + 3, NZ), lax.rem(z + 2, NZ)
    to_x = {"tp": ox * NZ + z}
    to_r = {"tp": xl * NZ + zr}
    to_l = {"tp": xl * NZ + zl}

    def cols(block):
        return pl.ds(pl.multiple_of(block * col_block, col_block), col_block)

    def w_copy(block):
        return pltpu.make_async_copy(
            w_hbm.at[:, cols(block)], w_v.at[:, cols(block)], w_sem.at[block]
        )

    own = pltpu.make_async_copy(og_hbm, og.at[xl, z], own_sem)
    own.start()

    @pl.loop(0, n_blocks)
    def _(block):
        w_copy(block).start()

    barrier = pltpu.get_barrier_semaphore()
    for peer in (to_x, to_r, to_l):
        pl.semaphore_signal(barrier, inc=1, device_id=peer, device_id_type=MESH)

    @pl.loop(1, n_ctx)
    def _(k):
        pl.semaphore_signal(
            barrier, inc=1, device_id={"ctx": lax.rem(me + k, n_ctx)}, device_id_type=MESH
        )

    pl.semaphore_wait(barrier, n_ctx + 2)

    def ag(index, src, dst, peer):
        return pltpu.make_async_remote_copy(
            src_ref=src,
            dst_ref=dst,
            send_sem=ag_s.at[index],
            recv_sem=ag_r.at[index],
            device_id=peer,
            device_id_type=MESH,
        )

    def relay(index, shard_x, shard_z, columns, peer):
        piece = og.at[shard_x, shard_z, :, columns]
        return ag(index, piece, piece, peer)

    all_a, all_b = pl.ds(0, half), pl.ds(half, half)
    a1, a2 = pl.ds(0, quarter), pl.ds(quarter, quarter)
    b1, b2 = pl.ds(half, quarter), pl.ds(half + quarter, quarter)

    first = [ag(i, og_hbm, og.at[xl, z], p) for i, p in enumerate((to_x, to_r, to_l))]
    for copy in first:
        copy.start()
    second = [
        relay(3, ox, z, all_a, to_r),
        relay(4, ox, z, all_a, to_l),
        relay(5, xl, zl, b1, to_r),
        relay(6, xl, zr, b2, to_l),
        relay(7, xl, zl, all_b, to_x),
        relay(8, xl, zr, all_b, to_x),
        relay(9, xl, zl, a1, to_r),
        relay(10, xl, zr, a2, to_l),
    ]
    third = [
        relay(11, xl, zo, all_b, to_x),
        relay(12, ox, zl, a1, to_r),
        relay(13, ox, zr, a2, to_l),
    ]

    lr_t = jnp.transpose(lr_ref[...])
    rate = jnp.exp(lr_t) / seq
    rate_t[...] = rate
    c_t[...] = jnp.transpose(res_ref[...]) * jnp.sqrt(2.0 * rate)
    for n in range(modes):
        row = pl.ds(n, 1)
        rate8[n] = jnp.broadcast_to(rate_t[row, :], (SUB, chans))
        c8[n] = jnp.broadcast_to(c_t[row, :], (SUB, chans))
    a8[...] = jnp.exp(-rate8[...])

    def lane(k):
        return pl.ds(k * LANE, LANE)

    for k in range(lanes):
        x32[k] = x_ref[:, lane(k)].astype(F32)

    place = lax.broadcasted_iota(jnp.int32, (modes, SUB, LANE), 1)
    place_f = place.astype(F32)
    span = float(steps)

    def at_step(ref, i, k):
        return ref[k, pl.ds(i, SUB, stride=steps), :]

    for k in range(lanes):
        a = a8[:, :, lane(k)]

        def grow(i, h, a=a, k=k):
            return a * h + at_step(x32, i, k)[None]

        end = lax.fori_loop(0, steps, grow, jnp.zeros((modes, SUB, LANE), F32), unroll=4)
        rk = rate8[:, :, lane(k)]
        for s in (1, 2, 4):
            moved = jnp.where(place >= s, pltpu.roll(end, s, 1), 0.0)
            end = end + jnp.exp(-(span * s) * rk) * moved
        ex8[:, :, lane(k)] = jnp.where(place >= 1, pltpu.roll(end, 1, 1), 0.0)
        s_send[:, lane(k)] = jnp.sum(jnp.where(place == SUB - 1, end, 0.0), axis=1)

    def ctx_copy(src, dst, sends, recvs, peer, sender):
        return pltpu.make_async_remote_copy(
            src_ref=src,
            dst_ref=dst,
            send_sem=sends.at[peer],
            recv_sem=recvs.at[sender],
            device_id={"ctx": peer},
            device_id_type=MESH,
        )

    def s_copy(peer, sender):
        return ctx_copy(s_send, s_recv.at[sender], s_ss, s_rs, peer, sender)

    def r_copy(peer, sender):
        return ctx_copy(r_send, r_recv.at[sender], r_ss, r_rs, peer, sender)

    @pl.loop(me + 1, n_ctx)
    def _(peer):
        s_copy(peer, me).start()

    for copy in first:
        copy.wait_recv()
    for copy in second:
        copy.start()

    far = jnp.exp(-float(tok) * rate_t[...])

    def join(sender, total):
        s_copy(0, sender).wait_recv()
        return far * total + s_recv[sender]

    st_t[...] = lax.fori_loop(0, me, join, jnp.zeros((modes, chans), F32))
    for n in range(modes):
        in8[n] = jnp.broadcast_to(st_t[pl.ds(n, 1), :], (SUB, chans))

    for k in range(lanes):
        a, c = a8[:, :, lane(k)], c8[:, :, lane(k)]
        skip = skip_ref[:, lane(k)]
        start = ex8[:, :, lane(k)] + jnp.exp(-span * place_f * rate8[:, :, lane(k)]) * in8[
            :, :, lane(k)
        ]

        def emit(i, h, a=a, c=c, skip=skip, k=k):
            now = at_step(x32, i, k)
            h = a * h + now[None]
            hall[i, :, :, lane(k)] = h
            y32[k, pl.ds(i, SUB, stride=steps), :] = jnp.sum(c * h, axis=0) + skip * now
            return h

        lax.fori_loop(0, steps, emit, start, unroll=2)
        mb[:, lane(k)] = y32[k].astype(BF16)

    for copy in second[:4]:
        copy.wait_recv()
    for copy in third:
        copy.start()

    def rs(index, src, dst, peer):
        return pltpu.make_async_remote_copy(
            src_ref=src,
            dst_ref=dst,
            send_sem=rs_s.at[index],
            recv_sem=rs_r.at[index],
            device_id=peer,
            device_id_type=MESH,
        )

    def project(block):
        w_copy(block).wait()
        p = jnp.dot(mb[...], w_v[:, cols(block)], preferred_element_type=F32)
        part[:, :, :, cols(block)] = p.astype(BF16).reshape(NX, NZ, rows, col_block)

    pl.loop(0, n_blocks // 2)(project)
    rs_x1 = rs(0, part.at[ox, :, :, all_a], bx1, to_x)
    rs_x1.start()
    pl.loop(n_blocks // 2, n_blocks)(project)
    rs_l1 = rs(1, part.at[:, zo, :, b1], bl1, to_r)
    rs_r1 = rs(2, part.at[:, zo, :, b2], br1, to_l)
    rs_l1.start()
    rs_r1.start()

    for copy in second[4:] + third:
        copy.wait_recv()
    own.wait()

    gacc[...] = jnp.zeros_like(gacc)

    @pl.loop(0, n_blocks)
    def _(block):
        gacc[...] += lax.dot_general(
            og[:, :, :, cols(block)].reshape(tok, col_block),
            w_v[:, cols(block)],
            (((1,), (1,)), ((), ())),
            preferred_element_type=F32,
        )

    for k in range(lanes):
        g32[k] = gacc[:, lane(k)].astype(BF16).astype(F32)
        a = a8[:, :, lane(k)]

        def back(i, h, a=a, k=k):
            return a * h + at_step(g32, steps - 1 - i, k)[None]

        end = lax.fori_loop(0, steps, back, jnp.zeros((modes, SUB, LANE), F32), unroll=4)
        rk = rate8[:, :, lane(k)]
        for s in (1, 2, 4):
            moved = jnp.where(place < SUB - s, pltpu.roll(end, SUB - s, 1), 0.0)
            end = end + jnp.exp(-(span * s) * rk) * moved
        ex8[:, :, lane(k)] = jnp.where(place < SUB - 1, pltpu.roll(end, SUB - 1, 1), 0.0)
        r_send[:, lane(k)] = jnp.sum(jnp.where(place == 0, end, 0.0), axis=1)

    @pl.loop(0, me)
    def _(peer):
        r_copy(peer, me).start()

    def merge(ref, got):
        ref[...] = (ref[...].astype(F32) + got[...].astype(F32)).astype(BF16)

    rs_x1.wait_recv()
    merge(part.at[xl, zo, :, all_a], bx1.at[zo])
    rs_al1 = rs(3, part.at[xl, zo, :, a1], al1, to_r)
    rs_ar1 = rs(4, part.at[xl, zo, :, a2], ar1, to_l)
    rs_al1.start()
    rs_ar1.start()
    rs_l1.wait_recv()
    merge(part.at[:, zr, :, b1], bl1)
    rs_l2 = rs(5, part.at[:, zr, :, all_b], bl2, to_r)
    rs_l2.start()
    rs_r1.wait_recv()
    merge(part.at[:, zl, :, b2], br1)
    rs_r2 = rs(6, part.at[:, zl, :, all_b], br2, to_l)
    rs_r2.start()
    merge(part.at[xl, zr, :, all_a], bx1.at[zr])
    merge(part.at[xl, zl, :, all_a], bx1.at[zl])

    def join_back(j, total):
        sender = n_ctx - 1 - j
        r_copy(0, sender).wait_recv()
        return far * total + r_recv[sender]

    st_t[...] = lax.fori_loop(
        0, n_ctx - 1 - me, join_back, jnp.zeros((modes, chans), F32)
    )
    for n in range(modes):
        in8[n] = jnp.broadcast_to(st_t[pl.ds(n, 1), :], (SUB, chans))

    rs_al1.wait_recv()
    merge(part.at[xl, zr, :, a1], al1)
    rs_al2 = rs(7, part.at[xl, zr, :, all_a], al2, to_r)
    rs_al2.start()
    rs_ar1.wait_recv()
    merge(part.at[xl, zl, :, a2], ar1)
    rs_ar2 = rs(8, part.at[xl, zl, :, all_a], ar2, to_l)
    rs_ar2.start()

    for k in range(lanes):
        a, c = a8[:, :, lane(k)], c8[:, :, lane(k)]
        skip = skip_ref[:, lane(k)]
        start = ex8[:, :, lane(k)] + jnp.exp(
            -span * (SUB - 1.0 - place_f) * rate8[:, :, lane(k)]
        ) * in8[:, :, lane(k)]
        g8[:, :, lane(k)] = jnp.zeros((modes, SUB, LANE), F32)
        m8[:, :, lane(k)] = jnp.zeros((modes, SUB, LANE), F32)

        def emit_back(j, carry, a=a, c=c, skip=skip, k=k):
            h, sk = carry
            i = steps - 1 - j
            now = at_step(g32, i, k)
            h = a * h + now[None]
            y32[k, pl.ds(i, SUB, stride=steps), :] = jnp.sum(c * h, axis=0) + skip * now
            held = hall[i, :, :, lane(k)]
            g8[:, :, lane(k)] += now[None] * held
            m8[:, :, lane(k)] += h * held
            return h, sk + now * at_step(x32, i, k)

        _, sk = lax.fori_loop(
            0, steps, emit_back, (start, jnp.zeros((SUB, LANE), F32)), unroll=2
        )
        red[:, pl.ds(k, 1), :] = jnp.sum(g8[:, :, lane(k)], axis=1, keepdims=True)
        red[:, pl.ds(lanes + k, 1), :] = jnp.sum(m8[:, :, lane(k)], axis=1, keepdims=True)
        sk = jnp.sum(sk, axis=0, keepdims=True)
        red[:, pl.ds(2 * lanes + k, 1), :] = jnp.broadcast_to(sk[None], (modes, 1, LANE))

    def p_copy(peer, sender):
        return ctx_copy(red.at[peer], rr.at[sender], p_ss, p_rs, peer, sender)

    def q_copy(peer, sender):
        return ctx_copy(fin.at[sender], fin.at[sender], q_ss, q_rs, peer, sender)

    def others(step):
        pl.loop(1, n_ctx)(lambda k: step(lax.rem(me + k, n_ctx)))

    others(lambda peer: p_copy(peer, me).start())
    for k in range(lanes):
        gi_ref[:, lane(k)] = y32[k].astype(BF16)
    rr[me] = red[me]

    rs_l2.wait_recv()
    rs_r2.wait_recv()

    def total3(ref, left, right):
        return ref[...].astype(F32) + left[...].astype(F32) + right[...].astype(F32)

    far_part = part.at[ox, z, :, all_b]
    far_part[...] = total3(far_part, bl2.at[ox], br2.at[ox]).astype(BF16)
    rs_x3 = rs(9, far_part, bx3, to_x)
    rs_x3.start()

    others(lambda peer: p_copy(0, peer).wait_recv())
    total = lax.fori_loop(1, n_ctx, lambda c, t: t + rr[c], rr[0])
    fin[me] = total[: 2 * lanes]
    others(lambda peer: q_copy(peer, me).start())
    scale = 1.0 / math.sqrt(seq)
    gskip_ref[...] = total[2 * lanes : 3 * lanes] * scale

    rs_al2.wait_recv()
    rs_ar2.wait_recv()
    out_ref[:, all_a] = (
        total3(part.at[xl, z, :, all_a], al2, ar2) + bx1[z].astype(F32)
    ).astype(BF16)
    rs_x3.wait_recv()
    out_ref[:, all_b] = (
        total3(part.at[xl, z, :, all_b], bl2.at[xl], br2.at[xl]) + bx3[...].astype(F32)
    ).astype(BF16)

    others(lambda peer: q_copy(0, peer).wait_recv())
    for k in range(lanes):
        rate = rate_t[:, lane(k)]
        gr = jnp.sum(fin[:, pl.ds(k, 1), :], axis=1)
        ml = jnp.sum(fin[:, pl.ds(lanes + k, 1), :], axis=1)
        here = pl.ds(k * LANE, LANE)
        gres_ref[here, :] = jnp.transpose(gr * (jnp.sqrt(2.0 * rate) * scale))
        glog_ref[here, :] = jnp.transpose(
            c_t[:, lane(k)] * ((0.5 + rate) * gr - rate * ml) * scale
        )

    for copy in first + second + third:
        copy.wait_send()
    for copy in (rs_x1, rs_l1, rs_r1, rs_al1, rs_ar1, rs_l2, rs_r2, rs_al2, rs_ar2, rs_x3):
        copy.wait_send()

    @pl.loop(me + 1, n_ctx)
    def _(peer):
        s_copy(peer, me).wait_send()

    @pl.loop(0, me)
    def _(peer):
        r_copy(peer, me).wait_send()

    others(lambda peer: p_copy(peer, me).wait_send())
    others(lambda peer: q_copy(peer, me).wait_send())


def per_device(inputs, residue, log_rate, skip, out_weight, out_grad):
    n_ctx = lax.axis_size("ctx")
    tok, chans = inputs.shape
    modes = residue.shape[1]
    dim = out_weight.shape[1]
    rows = tok // (NX * NZ)
    steps = tok // SUB
    lanes = chans // LANE
    half, quarter = dim // 2, dim // 4
    n_blocks = dim // min(1024, half)
    wide = (modes, SUB, chans)
    flat = (modes, chans)
    packed = -(-3 * lanes // SUB) * SUB
    vmem = pl.BlockSpec(memory_space=pltpu.VMEM)
    hbm = pl.BlockSpec(memory_space=pl.ANY)
    dma = pltpu.SemaphoreType.DMA
    out, gi, gres, glog, gskip = pl.pallas_call(
        functools.partial(kernel, tok * n_ctx, n_ctx),
        out_shape=(
            jax.ShapeDtypeStruct((rows, dim), BF16),
            jax.ShapeDtypeStruct((tok, chans), BF16),
            jax.ShapeDtypeStruct((chans, modes), F32),
            jax.ShapeDtypeStruct((chans, modes), F32),
            jax.ShapeDtypeStruct((lanes, LANE), F32),
        ),
        in_specs=[vmem, vmem, vmem, vmem, hbm, hbm],
        out_specs=(vmem,) * 5,
        scratch_shapes=[
            pltpu.VMEM((chans, dim), BF16),
            pltpu.VMEM((NX, NZ, rows, dim), BF16),
            pltpu.VMEM((NX, NZ, rows, dim), BF16),
            pltpu.VMEM((steps, *wide), F32),
            pltpu.VMEM((lanes, tok, LANE), F32),
            pltpu.VMEM((lanes, tok, LANE), F32),
            pltpu.VMEM((lanes, tok, LANE), F32),
            pltpu.VMEM((tok, chans), F32),
            pltpu.VMEM((tok, chans), BF16),
            pltpu.VMEM(flat, F32),
            pltpu.VMEM(flat, F32),
            pltpu.VMEM(wide, F32),
            pltpu.VMEM(wide, F32),
            pltpu.VMEM(wide, F32),
            pltpu.VMEM(wide, F32),
            pltpu.VMEM(wide, F32),
            pltpu.VMEM(flat, F32),
            pltpu.VMEM(flat, F32),
            pltpu.VMEM((n_ctx, *flat), F32),
            pltpu.VMEM(flat, F32),
            pltpu.VMEM((n_ctx, *flat), F32),
            pltpu.VMEM(wide, F32),
            pltpu.VMEM(wide, F32),
            pltpu.VMEM((SUB, chans), F32),
            pltpu.VMEM((modes, packed, LANE), F32),
            pltpu.VMEM((n_ctx, packed, LANE), F32),
            pltpu.VMEM((n_ctx, 2 * lanes, LANE), F32),
            pltpu.VMEM((NZ, rows, half), BF16),
            pltpu.VMEM((NX, rows, quarter), BF16),
            pltpu.VMEM((NX, rows, quarter), BF16),
            pltpu.VMEM((NX, rows, half), BF16),
            pltpu.VMEM((NX, rows, half), BF16),
            pltpu.VMEM((rows, half), BF16),
            pltpu.VMEM((rows, quarter), BF16),
            pltpu.VMEM((rows, quarter), BF16),
            pltpu.VMEM((rows, half), BF16),
            pltpu.VMEM((rows, half), BF16),
            dma((n_blocks,)),
            dma,
            dma((14,)),
            dma((14,)),
            dma((10,)),
            dma((10,)),
            *[dma((n_ctx,)) for _ in range(8)],
        ],
        compiler_params=pltpu.CompilerParams(
            collective_id=0, has_side_effects=True, vmem_limit_bytes=48 * 1024 * 1024
        ),
    )(inputs, residue, log_rate, skip.reshape(1, chans), out_weight, out_grad)
    return out, gi, gres, glog, gskip.reshape(chans)


def solution(mesh):
    return jax.shard_map(
        per_device,
        mesh=mesh,
        in_specs=(
            P("ctx", "tp"),
            P("tp", None),
            P("tp", None),
            P("tp"),
            P("tp", None),
            P(("ctx", "tp"), None),
        ),
        out_specs=(P(("ctx", "tp"), None), P("ctx", "tp"), P("tp", None), P("tp", None), P("tp")),
        check_vma=False,
    )
```

profile of v0, /device:TPU:1, one launch (start us, length us, event | category | flops | bytes accessed | tf_op | source)
XLA Modules:
  0.0 70.8 jit_solution(10423732077608738652)
XLA Ops:
  0.6 0.9 %copy.11.res_ref = f32[512,16]{1,0:T(8,128)S(1)} copy(f32[512,16]{0,1:T(8,128)} %param.7) | data formatting | bytes 65536 | tf_op args[1]
  1.5 0.9 %copy.12.lr_ref = f32[512,16]{1,0:T(8,128)S(1)} copy(f32[512,16]{0,1:T(8,128)} %param.8) | data formatting | bytes 65536 | tf_op args[2]
  2.4 0.0 copy-start
  2.4 0.9 %copy-done = bf16[16,8192]{1,0:T(8,128)(2,1)S(1)} copy-done((bf16[16,8192]{1,0:T(8,128)(2,1)S(1)}, bf16[16,8192]{1,0:T(8,128)(2,1)}, u32[]{:S(2)}) %copy-start) | copy-done | bytes 262168
  3.4 0.0 copy-start.1
  3.4 0.9 %copy-done.1 = bf16[128,512]{1,0:T(8,128)(2,1)S(1)} copy-done((bf16[128,512]{1,0:T(8,128)(2,1)S(1)}, bf16[128,512]{1,0:T(8,128)(2,1)}, u32[]{:S(2)}) %copy-start.1) | copy-done | bytes 131096
  4.3 0.0 copy-start.2
  4.3 0.7 copy-done.2
  5.0 62.5 %shard_map.101 = (bf16[16,8192]{1,0:T(8,128)(2,1)S(1)}, bf16[128,512]{1,0:T(8,128)(2,1)S(1)}, f32[512,16]{1,0:T(8,128)S(1)}, f32[512,16]{1,0:T(8,128)S(1)}, f32[4,128]{1,0:T(4,128)S(1)}) custom-call(bf16[128,512]{1,0:T(8,128)(2,1)S(1)} %copy-done.1, f32[512,16]{1,0:T(8,128)S(1)} %copy.11.res_ref, f32[512,16]{1,0:T(8,128)S(1)} %copy.12.lr_ref, ...), custom_call_target="tpu_custom_call" | custom-call | tf_op jit(solution)/shard_map/pallas_call | solution.py:474
  67.4 0.7 %copy.13 = f32[512,16]{0,1:T(8,128)} copy(f32[512,16]{1,0:T(8,128)S(1)} %get-tuple-element.17) | data formatting | bytes 65536
  68.2 0.7 %copy.14 = f32[512,16]{0,1:T(8,128)} copy(f32[512,16]{1,0:T(8,128)S(1)} %get-tuple-element.18) | data formatting | bytes 65536
  68.9 0.7 copy.18
  69.6 0.7 copy.19
  70.2 0.6 copy.20
Async XLA Ops:
  2.4 1.0 %copy-start = (bf16[16,8192]{1,0:T(8,128)(2,1)S(1)}, bf16[16,8192]{1,0:T(8,128)(2,1)}, u32[]{:S(2)}) copy-start(bf16[16,8192]{1,0:T(8,128)(2,1)} %og_hbm.1) | copy-start | bytes 786436
  3.4 0.9 %copy-start.1 = (bf16[128,512]{1,0:T(8,128)(2,1)S(1)}, bf16[128,512]{1,0:T(8,128)(2,1)}, u32[]{:S(2)}) copy-start(bf16[128,512]{1,0:T(8,128)(2,1)} %x_ref.1) | copy-start | bytes 393220
  4.3 0.7 copy-start.2
where the time goes:
time: 71.1 us; the launch traced here: 70.8 us
  Pallas kernels  62.5 us (88%)
  local copies, waits for them, and re-layouts  7.67 us (11%)
    pallas_call x1, Pallas kernels, per_device(): pl.pallas_call(functools.partial(kernel, tok * n_ctx, n_ctx), out_shape=(...  62.5 us
    unnamed x13, local copies, waits for them, and re-layouts  7.67 us

commit v1 on v0

v1 whole, which is shorter than its diff:
```python
import functools
import math

import jax
import jax.numpy as jnp
from jax import lax
from jax.experimental import pallas as pl
from jax.experimental.pallas import tpu as pltpu
from jax.sharding import PartitionSpec as P

MESH = pl.DeviceIdType.MESH
F32 = jnp.float32
BF16 = jnp.bfloat16
SUB = 8
LANE = 128
NX, NZ = 2, 4
A_PIECES, B_PIECES = 4, 2


def kernel(
    seq,
    n_ctx,
    x_hbm,
    res_hbm,
    lr_hbm,
    skip_hbm,
    w_hbm,
    og_hbm,
    out_ref,
    gi_ref,
    gres_ref,
    glog_ref,
    gskip_ref,
    x_ref,
    res_ref,
    lr_ref,
    skip_ref,
    w_v,
    og,
    part,
    hall,
    x32,
    y32,
    g32,
    gacc,
    mb,
    rate_t,
    c_t,
    far4,
    rate8,
    a8,
    c8,
    ex8,
    in8,
    v8,
    st_t,
    s_send,
    s_recv,
    r_send,
    r_recv,
    red,
    rr,
    fin,
    bx1,
    al1,
    ar1,
    al2,
    ar2,
    bl1,
    br1,
    bl2,
    br2,
    bx3,
    in_sem,
    w_sem,
    ag_s,
    ag_r,
    rs_s,
    rs_r,
    s_ss,
    s_rs,
    r_ss,
    r_rs,
    p_ss,
    p_rs,
    q_ss,
    q_rs,
):
    tok, chans = x_ref.shape
    modes = res_ref.shape[0]
    dim = w_v.shape[1]
    rows = tok // (NX * NZ)
    steps = tok // SUB
    lanes = chans // LANE
    half, quarter = dim // 2, dim // 4
    a_cols, b_cols = half // A_PIECES, half // B_PIECES
    n_blocks = dim // a_cols

    me = lax.axis_index("ctx")
    tp = lax.axis_index("tp")
    xl, z = tp // NZ, lax.rem(tp, NZ)
    ox = 1 - xl
    zr, zl, zo = lax.rem(z + 1, NZ), lax.rem(z + 3, NZ), lax.rem(z + 2, NZ)
    to_x = {"tp": ox * NZ + z}
    to_r = {"tp": xl * NZ + zr}
    to_l = {"tp": xl * NZ + zl}

    def cols(block):
        return pl.ds(pl.multiple_of(block * a_cols, a_cols), a_cols)

    def w_copy(block):
        return pltpu.make_async_copy(
            w_hbm.at[:, cols(block)], w_v.at[:, cols(block)], w_sem.at[block]
        )

    ins = [
        pltpu.make_async_copy(src, dst, in_sem.at[i])
        for i, (src, dst) in enumerate(
            (
                (lr_hbm, lr_ref),
                (res_hbm, res_ref),
                (x_hbm, x_ref),
                (skip_hbm, skip_ref),
                (og_hbm, og.at[xl, z]),
            )
        )
    ]
    for copy in ins:
        copy.start()
    barrier = pltpu.get_barrier_semaphore()
    for peer in (to_x, to_r, to_l):
        pl.semaphore_signal(barrier, inc=1, device_id=peer, device_id_type=MESH)

    @pl.loop(1, n_ctx)
    def _(k):
        pl.semaphore_signal(
            barrier, inc=1, device_id={"ctx": lax.rem(me + k, n_ctx)}, device_id_type=MESH
        )

    @pl.loop(0, n_blocks)
    def _(block):
        w_copy(block).start()

    for copy in ins[:4]:
        copy.wait()
    rate = jnp.exp(lr_ref[...]) / seq
    rate_t[...] = rate
    c_t[...] = res_ref[...] * jnp.sqrt(2.0 * rate)
    far = jnp.exp(-float(tok) * rate)
    for n in range(modes):
        row = pl.ds(n, 1)
        rate8[n] = jnp.broadcast_to(rate_t[row, :], (SUB, chans))
        c8[n] = jnp.broadcast_to(c_t[row, :], (SUB, chans))
    a8[...] = jnp.exp(-rate8[...])

    def lane(k):
        return pl.ds(k * LANE, LANE)

    for k in range(lanes):
        x32[k] = x_ref[:, lane(k)].astype(F32)
        far4[:, pl.ds(k, 1), :] = far[:, k * LANE : (k + 1) * LANE][:, None, :]

    place = lax.broadcasted_iota(jnp.int32, (modes, SUB, LANE), 1)
    place_f = place.astype(F32)
    span = float(steps)
    zero = jnp.zeros((modes, SUB, LANE), F32)

    def at_step(ref, i, k):
        return ref[k, pl.ds(i, SUB, stride=steps), :]

    for k in range(lanes):
        a = a8[:, :, lane(k)]

        def grow(i, h, a=a, k=k):
            return a * h + at_step(x32, i, k)[None]

        end = lax.fori_loop(0, steps, grow, zero, unroll=4)
        rk = rate8[:, :, lane(k)]
        for s in (1, 2, 4):
            moved = jnp.where(place >= s, pltpu.roll(end, s, 1), 0.0)
            end = end + jnp.exp(-(span * s) * rk) * moved
        ex8[:, :, lane(k)] = jnp.where(place >= 1, pltpu.roll(end, 1, 1), 0.0)
        s_send[:, lane(k)] = jnp.sum(jnp.where(place == SUB - 1, end, 0.0), axis=1).astype(BF16)

    pl.semaphore_wait(barrier, n_ctx + 2)

    def ctx_copy(src, dst, sends, recvs, peer, sender):
        return pltpu.make_async_remote_copy(
            src_ref=src,
            dst_ref=dst,
            send_sem=sends.at[peer],
            recv_sem=recvs.at[sender],
            device_id={"ctx": peer},
            device_id_type=MESH,
        )

    def s_copy(peer, sender):
        return ctx_copy(s_send, s_recv.at[sender], s_ss, s_rs, peer, sender)

    def r_copy(peer, sender):
        return ctx_copy(r_send, r_recv.at[sender], r_ss, r_rs, peer, sender)

    def p_copy(peer, sender):
        return ctx_copy(red.at[peer], rr.at[sender], p_ss, p_rs, peer, sender)

    def q_copy(peer, sender):
        return ctx_copy(fin.at[sender], fin.at[sender], q_ss, q_rs, peer, sender)

    def others(step):
        pl.loop(1, n_ctx)(lambda k: step(lax.rem(me + k, n_ctx)))

    @pl.loop(me + 1, n_ctx)
    def _(peer):
        s_copy(peer, me).start()

    tags = iter(range(100))

    def ag(src, dst, peer):
        index = next(tags)
        return pltpu.make_async_remote_copy(
            src_ref=src,
            dst_ref=dst,
            send_sem=ag_s.at[index],
            recv_sem=ag_r.at[index],
            device_id=peer,
            device_id_type=MESH,
        )

    def relay(shard_x, shard_z, columns, peer):
        piece = og.at[shard_x, shard_z, :, columns]
        return ag(piece, piece, peer)

    def mine(columns, peer):
        return ag(og_hbm.at[:, columns], og.at[xl, z, :, columns], peer)

    all_a, all_b = pl.ds(0, half), pl.ds(half, half)
    a1, a2 = pl.ds(0, quarter), pl.ds(quarter, quarter)
    b1, b2 = pl.ds(half, quarter), pl.ds(half + quarter, quarter)

    x_a, r_b, l_b = mine(all_a, to_x), mine(all_b, to_r), mine(all_b, to_l)
    x_b, r_a, l_a = mine(all_b, to_x), mine(all_a, to_r), mine(all_a, to_l)
    gathers = [x_a, r_b, l_b, x_b, r_a, l_a]
    for copy in gathers:
        copy.start()

    x_a.wait_recv()
    r_xa, l_xa = relay(ox, z, all_a, to_r), relay(ox, z, all_a, to_l)
    r_xa.start()
    l_xa.start()
    r_b.wait_recv()
    l_b.wait_recv()
    x_lb, x_rb = relay(xl, zl, all_b, to_x), relay(xl, zr, all_b, to_x)
    r_ob, l_ob = relay(xl, zl, b1, to_r), relay(xl, zr, b2, to_l)
    more = [r_ob, l_ob, x_lb, x_rb]
    for copy in more:
        copy.start()
    gathers += [r_xa, l_xa] + more

    def join(sender, total):
        s_copy(0, sender).wait_recv()
        return far * total + s_recv[sender].astype(F32)

    st_t[...] = lax.fori_loop(0, me, join, jnp.zeros((modes, chans), F32))
    for n in range(modes):
        in8[n] = jnp.broadcast_to(st_t[pl.ds(n, 1), :], (SUB, chans))

    for k in range(lanes):
        a, c = a8[:, :, lane(k)], c8[:, :, lane(k)]
        skip = skip_ref[:, lane(k)]
        start = ex8[:, :, lane(k)] + jnp.exp(-span * place_f * rate8[:, :, lane(k)]) * in8[
            :, :, lane(k)
        ]

        def emit(i, h, a=a, c=c, skip=skip, k=k):
            now = at_step(x32, i, k)
            h = a * h + now[None]
            hall[i, :, :, lane(k)] = h
            y32[k, pl.ds(i, SUB, stride=steps), :] = jnp.sum(c * h, axis=0) + skip * now
            return h

        lax.fori_loop(0, steps, emit, start, unroll=2)
        mb[:, lane(k)] = y32[k].astype(BF16)

    r_a.wait_recv()
    l_a.wait_recv()
    r_oa, l_oa = relay(xl, zl, a1, to_r), relay(xl, zr, a2, to_l)
    r_oa.start()
    l_oa.start()
    r_xa.wait_recv()
    l_xa.wait_recv()
    r_oxa, l_oxa = relay(ox, zl, a1, to_r), relay(ox, zr, a2, to_l)
    r_oxa.start()
    l_oxa.start()
    r_ob.wait_recv()
    l_ob.wait_recv()
    x_ob = relay(xl, zo, all_b, to_x)
    x_ob.start()
    gathers += [r_oa, l_oa, r_oxa, l_oxa, x_ob]

    sums = iter(range(100))
    reduces = []

    def rs(src, dst, peer):
        index = next(sums)
        copy = pltpu.make_async_remote_copy(
            src_ref=src,
            dst_ref=dst,
            send_sem=rs_s.at[index],
            recv_sem=rs_r.at[index],
            device_id=peer,
            device_id_type=MESH,
        )
        copy.start()
        reduces.append(copy)
        return copy

    def project(block):
        w_copy(block).wait()
        p = jnp.dot(mb[...], w_v[:, cols(block)], preferred_element_type=F32)
        part[:, :, :, cols(block)] = p.astype(BF16).reshape(NX, NZ, rows, a_cols)

    def a_span(i):
        return pl.ds(i * a_cols, a_cols)

    def a_halves(i):
        h = a_cols // 2
        return pl.ds(i * a_cols, h), pl.ds(i * a_cols + h, h)

    def b_span(i):
        return pl.ds(half + i * b_cols, b_cols)

    def b_halves(i):
        h = b_cols // 2
        return pl.ds(half + i * b_cols, h), pl.ds(half + i * b_cols + h, h)

    rs_x1 = []
    for i in range(A_PIECES):
        project(i)
        rs_x1.append(rs(part.at[ox, :, :, a_span(i)], bx1.at[i], to_x))
    rs_l1, rs_r1 = [], []
    for i in range(B_PIECES):
        per = A_PIECES // B_PIECES
        pl.loop(A_PIECES + i * per, A_PIECES + (i + 1) * per)(project)
        h1, h2 = b_halves(i)
        rs_l1.append(rs(part.at[:, zo, :, h1], bl1.at[i], to_r))
        rs_r1.append(rs(part.at[:, zo, :, h2], br1.at[i], to_l))

    for k in range(lanes):
        a = a8[:, :, lane(k)]

        def lift(i, v, a=a, k=k):
            return a * v + hall[i, :, :, lane(k)]

        v8[:, :, lane(k)] = a * lax.fori_loop(0, steps, lift, zero, unroll=4)

    x_a_parts = [r_oa, l_oa, r_oxa, l_oxa]
    for copy in x_a_parts:
        copy.wait_recv()
    ins[4].wait()

    gacc[...] = jnp.zeros_like(gacc)

    def project_back(block):
        gacc[...] += lax.dot_general(
            og[:, :, :, cols(block)].reshape(tok, a_cols),
            w_v[:, cols(block)],
            (((1,), (1,)), ((), ())),
            preferred_element_type=F32,
        )

    pl.loop(0, n_blocks // 2)(project_back)

    for copy in (x_b, x_lb, x_rb, x_ob):
        copy.wait_recv()

    pl.loop(n_blocks // 2, n_blocks)(project_back)

    for k in range(lanes):
        g32[k] = gacc[:, lane(k)].astype(BF16).astype(F32)
        lv = lane(k)
        hm = modes // 2
        for m0 in (0, hm):
            ms = pl.ds(m0, hm)
            a = a8[ms, :, lv]
            zh = jnp.zeros((hm, SUB, LANE), F32)

            def back(j, carry, a=a, k=k, lv=lv, ms=ms):
                h, gs, mloc = carry
                i = steps - 1 - j
                now = at_step(g32, i, k)[None]
                held = hall[i, ms, :, lv]
                h = a * h + now
                return h, gs + now * held, mloc + h * held

            end, gs, mloc = lax.fori_loop(0, steps, back, (zh, zh, zh), unroll=2)

            v = v8[ms, :, lv]
            pm = place[:hm]
            rk = rate8[ms, :, lv]
            for s in (1, 2, 4):
                moved = jnp.where(pm < SUB - s, pltpu.roll(end, SUB - s, 1), 0.0)
                end = end + jnp.exp(-(span * s) * rk) * moved
            ex = jnp.where(pm < SUB - 1, pltpu.roll(end, SUB - 1, 1), 0.0)
            ex8[ms, :, lv] = ex
            u = jnp.exp(-span * (SUB - 1.0 - place_f[:hm]) * rk) * v
            first = jnp.where(pm == 0, end, 0.0)
            r_send[ms, lv] = jnp.sum(first, axis=1).astype(BF16)
            for at, value in enumerate((gs, mloc + ex * v, u, first)):
                red[ms, pl.ds(at * lanes + k, 1), :] = jnp.sum(value, axis=1, keepdims=True)
        sk = jnp.sum(g32[k] * x32[k], axis=0, keepdims=True)
        red[:, pl.ds(4 * lanes + k, 1), :] = jnp.broadcast_to(sk[None], (modes, 1, LANE))

    others(lambda peer: p_copy(peer, me).start())

    @pl.loop(0, me)
    def _(peer):
        r_copy(peer, me).start()

    rr[me] = red[me]

    def merge(ref, got):
        ref[...] = (ref[...].astype(F32) + got[...].astype(F32)).astype(BF16)

    rs_l2, rs_r2 = [], []
    for i in range(B_PIECES):
        h1, h2 = b_halves(i)
        rs_l1[i].wait_recv()
        merge(part.at[:, zr, :, h1], bl1.at[i])
        rs_l2.append(rs(part.at[:, zr, :, b_span(i)], bl2.at[i], to_r))
        rs_r1[i].wait_recv()
        merge(part.at[:, zl, :, h2], br1.at[i])
        rs_r2.append(rs(part.at[:, zl, :, b_span(i)], br2.at[i], to_l))

    rs_al1, rs_ar1, rs_al2, rs_ar2 = [], [], [], []

    def take_x1(i):
        rs_x1[i].wait_recv()
        h1, h2 = a_halves(i)
        merge(part.at[xl, zo, :, a_span(i)], bx1.at[i, zo])
        rs_al1.append(rs(part.at[xl, zo, :, h1], al1.at[i], to_r))
        rs_ar1.append(rs(part.at[xl, zo, :, h2], ar1.at[i], to_l))
        merge(part.at[xl, zr, :, a_span(i)], bx1.at[i, zr])
        merge(part.at[xl, zl, :, a_span(i)], bx1.at[i, zl])

    def take_z1(i):
        h1, h2 = a_halves(i)
        rs_al1[i].wait_recv()
        merge(part.at[xl, zr, :, h1], al1.at[i])
        rs_al2.append(rs(part.at[xl, zr, :, a_span(i)], al2.at[i], to_r))
        rs_ar1[i].wait_recv()
        merge(part.at[xl, zl, :, h2], ar1.at[i])
        rs_ar2.append(rs(part.at[xl, zl, :, a_span(i)], ar2.at[i], to_l))

    for i in range(A_PIECES // 2):
        take_x1(i)

    def join_back(j, total):
        sender = n_ctx - 1 - j
        r_copy(0, sender).wait_recv()
        return far * total + r_recv[sender].astype(F32)

    st_t[...] = lax.fori_loop(0, n_ctx - 1 - me, join_back, jnp.zeros((modes, chans), F32))
    for n in range(modes):
        in8[n] = jnp.broadcast_to(st_t[pl.ds(n, 1), :], (SUB, chans))

    for k in range(lanes):
        a, c = a8[:, :, lane(k)], c8[:, :, lane(k)]
        skip = skip_ref[:, lane(k)]
        start = ex8[:, :, lane(k)] + jnp.exp(
            -span * (SUB - 1.0 - place_f) * rate8[:, :, lane(k)]
        ) * in8[:, :, lane(k)]

        def emit_back(j, h, a=a, c=c, skip=skip, k=k):
            i = steps - 1 - j
            now = at_step(g32, i, k)
            h = a * h + now[None]
            y32[k, pl.ds(i, SUB, stride=steps), :] = jnp.sum(c * h, axis=0) + skip * now
            return h

        lax.fori_loop(0, steps, emit_back, start, unroll=2)
        gi_ref[:, lane(k)] = y32[k].astype(BF16)

    for i in range(A_PIECES // 2, A_PIECES):
        take_x1(i)

    for i in range(A_PIECES // 2):
        take_z1(i)

    others(lambda peer: p_copy(0, peer).wait_recv())

    far_me = far4[me]

    def owner(j, carry):
        lam, gsum, msum, ksum = carry
        sender = n_ctx - 1 - j
        got = rr[sender]
        gsum = gsum + got[:lanes]
        msum = msum + got[lanes : 2 * lanes] + lam * got[2 * lanes : 3 * lanes]
        ksum = ksum + got[4 * lanes : 5 * lanes]
        return far_me * lam + got[3 * lanes : 4 * lanes], gsum, msum, ksum

    zl4 = jnp.zeros((lanes, LANE), F32)
    _, gsum, msum, ksum = lax.fori_loop(0, n_ctx, owner, (zl4, zl4, zl4, zl4))
    fin[me, pl.ds(0, lanes), :] = gsum
    fin[me, pl.ds(lanes, lanes), :] = msum
    others(lambda peer: q_copy(peer, me).start())
    scale = 1.0 / math.sqrt(seq)
    gskip_ref[...] = ksum * scale

    def total3(ref, left, right):
        return ref[...].astype(F32) + left[...].astype(F32) + right[...].astype(F32)

    rs_x3 = []
    for i in range(B_PIECES):
        rs_l2[i].wait_recv()
        rs_r2[i].wait_recv()
        far_part = part.at[ox, z, :, b_span(i)]
        far_part[...] = total3(far_part, bl2.at[i, ox], br2.at[i, ox]).astype(BF16)
        rs_x3.append(rs(far_part, bx3.at[i], to_x))

    for i in range(A_PIECES // 2, A_PIECES):
        take_z1(i)

    for i in range(A_PIECES):
        rs_al2[i].wait_recv()
        rs_ar2[i].wait_recv()
        out_ref[:, a_span(i)] = (
            total3(part.at[xl, z, :, a_span(i)], al2.at[i], ar2.at[i]) + bx1[i, z].astype(F32)
        ).astype(BF16)

    others(lambda peer: q_copy(0, peer).wait_recv())

    for k in range(lanes):
        rate = rate_t[:, lane(k)]
        gr = jnp.sum(fin[:, pl.ds(k, 1), :], axis=1)
        ml = jnp.sum(fin[:, pl.ds(lanes + k, 1), :], axis=1)
        gres_ref[:, lane(k)] = gr * (jnp.sqrt(2.0 * rate) * scale)
        glog_ref[:, lane(k)] = c_t[:, lane(k)] * ((0.5 + rate) * gr - rate * ml) * scale

    for i in range(B_PIECES):
        rs_x3[i].wait_recv()
        out_ref[:, b_span(i)] = (
            total3(part.at[xl, z, :, b_span(i)], bl2.at[i, xl], br2.at[i, xl])
            + bx3[i].astype(F32)
        ).astype(BF16)

    for copy in gathers + reduces:
        copy.wait_send()

    @pl.loop(me + 1, n_ctx)
    def _(peer):
        s_copy(peer, me).wait_send()

    @pl.loop(0, me)
    def _(peer):
        r_copy(peer, me).wait_send()

    others(lambda peer: p_copy(peer, me).wait_send())
    others(lambda peer: q_copy(peer, me).wait_send())


def store(*refs):
    n = len(refs) // 2
    copies = [
        pltpu.make_async_copy(refs[i], refs[n + i], refs[-1].at[i]) for i in range(n)
    ]
    for copy in copies:
        copy.start()
    for copy in copies:
        copy.wait()


def per_device(inputs, residue, log_rate, skip, out_weight, out_grad):
    n_ctx = lax.axis_size("ctx")
    tok, chans = inputs.shape
    modes = residue.shape[1]
    dim = out_weight.shape[1]
    rows = tok // (NX * NZ)
    steps = tok // SUB
    lanes = chans // LANE
    half = dim // 2
    a_cols, b_cols = half // A_PIECES, half // B_PIECES
    n_blocks = dim // a_cols
    wide = (modes, SUB, chans)
    flat = (modes, chans)
    packed = -(-5 * lanes // SUB) * SUB
    vmem = pl.BlockSpec(memory_space=pltpu.VMEM)
    anywhere = pl.BlockSpec(memory_space=pl.ANY)
    dma = pltpu.SemaphoreType.DMA
    results = (
        jax.ShapeDtypeStruct((rows, dim), BF16),
        jax.ShapeDtypeStruct((tok, chans), BF16),
        jax.ShapeDtypeStruct(flat, F32),
        jax.ShapeDtypeStruct(flat, F32),
        jax.ShapeDtypeStruct((lanes, LANE), F32),
    )
    held = pl.pallas_call(
        functools.partial(kernel, tok * n_ctx, n_ctx),
        out_shape=results,
        in_specs=[anywhere] * 6,
        out_specs=(vmem,) * 5,
        scratch_shapes=[
            pltpu.VMEM((tok, chans), BF16),
            pltpu.VMEM(flat, F32),
            pltpu.VMEM(flat, F32),
            pltpu.VMEM((1, chans), F32),
            pltpu.VMEM((chans, dim), BF16),
            pltpu.VMEM((NX, NZ, rows, dim), BF16),
            pltpu.VMEM((NX, NZ, rows, dim), BF16),
            pltpu.VMEM((steps, *wide), F32),
            pltpu.VMEM((lanes, tok, LANE), F32),
            pltpu.VMEM((lanes, tok, LANE), F32),
            pltpu.VMEM((lanes, tok, LANE), F32),
            pltpu.VMEM((tok, chans), F32),
            pltpu.VMEM((tok, chans), BF16),
            pltpu.VMEM(flat, F32),
            pltpu.VMEM(flat, F32),
            pltpu.VMEM((modes, lanes, LANE), F32),
            pltpu.VMEM(wide, F32),
            pltpu.VMEM(wide, F32),
            pltpu.VMEM(wide, F32),
            pltpu.VMEM(wide, F32),
            pltpu.VMEM(wide, F32),
            pltpu.VMEM(wide, F32),
            pltpu.VMEM(flat, F32),
            pltpu.VMEM(flat, BF16),
            pltpu.VMEM((n_ctx, *flat), BF16),
            pltpu.VMEM(flat, BF16),
            pltpu.VMEM((n_ctx, *flat), BF16),
            pltpu.VMEM((modes, packed, LANE), F32),
            pltpu.VMEM((n_ctx, packed, LANE), F32),
            pltpu.VMEM((n_ctx, 2 * lanes, LANE), F32),
            pltpu.VMEM((A_PIECES, NZ, rows, a_cols), BF16),
            pltpu.VMEM((A_PIECES, rows, a_cols // 2), BF16),
            pltpu.VMEM((A_PIECES, rows, a_cols // 2), BF16),
            pltpu.VMEM((A_PIECES, rows, a_cols), BF16),
            pltpu.VMEM((A_PIECES, rows, a_cols), BF16),
            pltpu.VMEM((B_PIECES, NX, rows, b_cols // 2), BF16),
            pltpu.VMEM((B_PIECES, NX, rows, b_cols // 2), BF16),
            pltpu.VMEM((B_PIECES, NX, rows, b_cols), BF16),
            pltpu.VMEM((B_PIECES, NX, rows, b_cols), BF16),
            pltpu.VMEM((B_PIECES, rows, b_cols), BF16),
            dma((5,)),
            dma((n_blocks,)),
            dma((17,)),
            dma((17,)),
            dma((5 * (A_PIECES + B_PIECES),)),
            dma((5 * (A_PIECES + B_PIECES),)),
            *[dma((n_ctx,)) for _ in range(8)],
        ],
        compiler_params=pltpu.CompilerParams(
            collective_id=0, has_side_effects=True, vmem_limit_bytes=56 * 1024 * 1024
        ),
    )(inputs, residue.T, log_rate.T, skip.reshape(1, chans), out_weight, out_grad)
    out, gi, gres, glog, gskip = pl.pallas_call(
        store,
        out_shape=results,
        in_specs=[vmem] * 5,
        out_specs=(anywhere,) * 5,
        scratch_shapes=[dma((5,))],
    )(*held)
    return out, gi, gres.T, glog.T, gskip.reshape(chans)


def solution(mesh):
    return jax.shard_map(
        per_device,
        mesh=mesh,
        in_specs=(
            P("ctx", "tp"),
            P("tp", None),
            P("tp", None),
            P("tp"),
            P("tp", None),
            P(("ctx", "tp"), None),
        ),
        out_specs=(P(("ctx", "tp"), None), P("ctx", "tp"), P("tp", None), P("tp", None), P("tp")),
        check_vma=False,
    )
```

time: 71.1 us -> 55 us (0.77)
  Pallas kernels: 62.5 us -> 54.2 us
  local copies, waits for them, and re-layouts: 7.67 us -> 0 us
    pallas_call x1 -> x2, Pallas kernels: 62.5 us -> 54.2 us  [the longest x1 52.3 us: per_device(): pl.pallas_call(functools.partial(kernel, tok * n_ctx, n_ctx), out_shape=r...]
    unnamed x13 -> x0, local copies, waits for them, and re-layouts: 7.67 us -> none
where the time goes in v1:
time: 55 us; the launch traced here: 54.8 us
  Pallas kernels  54.2 us (99%)
  between operations  0.64 us (1%)
    pallas_call x1, Pallas kernels, per_device(): pl.pallas_call(functools.partial(kernel, tok * n_ctx, n_ctx), out_shape=r...  52.3 us
    pallas_call x1, Pallas kernels, per_device(): pl.pallas_call(store, out_shape=results, in_specs=[vmem] * 5, out_specs=(...  1.85 us

profile of v1, /device:TPU:1, one launch (start us, length us, event | category | flops | bytes accessed | tf_op | source)
XLA Modules:
  0.0 54.8 jit_solution(12944077491618668789)
XLA Ops:
  0.6 52.3 %shard_map.101 = (bf16[16,8192]{1,0:T(8,128)(2,1)}, bf16[128,512]{1,0:T(8,128)(2,1)}, f32[16,512]{1,0:T(8,128)}, f32[16,512]{1,0:T(8,128)}, f32[4,128]{1,0:T(4,128)}) custom-call(bf16[128,512]{1,0:T(8,128)(2,1)} %x_hbm.1, f32[16,512]{1,0:T(8,128)} %bitcast.6, f32[16,512]{1,0:T(8,128)} %bitcast.7, f32[1,512]{1,0:T(1,128)} %bitcast.8, ...), custom_call_target="tpu_custom_call" | custom-call | tf_op jit(solution)/shard_map/pallas_call | solution.py:597
  53.0 1.8 %shard_map.102 = (bf16[16,8192]{1,0:T(8,128)(2,1)}, bf16[128,512]{1,0:T(8,128)(2,1)}, f32[16,512]{1,0:T(8,128)}, f32[16,512]{1,0:T(8,128)}, f32[4,128]{1,0:T(4,128)}) custom-call(bf16[16,8192]{1,0:T(8,128)(2,1)} %get-tuple-element.15.refs_0_, bf16[128,512]{1,0:T(8,128)(2,1)} %get-tuple-element.16.refs_1_, f32[16,512]{1,0:T(8,128)} %get-tuple-element.17.refs_2_, ...), custom_call_target="tpu_custom_call" | custom-call | tf_op jit(solution)/shard_map/pallas_call | solution.py:655

commit v2 on v1

v2 whole, which is shorter than its diff:
```python
import functools
import math

import jax
import jax.numpy as jnp
from jax import lax
from jax.experimental import pallas as pl
from jax.experimental.pallas import tpu as pltpu
from jax.sharding import PartitionSpec as P

MESH = pl.DeviceIdType.MESH
F32 = jnp.float32
BF16 = jnp.bfloat16
SUB = 8
LANE = 128
NX, NZ = 2, 4
PIECES, A_PIECES, B_PIECES = 8, 2, 3


def kernel(
    seq,
    n_ctx,
    x_hbm,
    res_hbm,
    lr_hbm,
    skip_hbm,
    w_hbm,
    og_hbm,
    out_hbm,
    gi_hbm,
    gres_hbm,
    glog_hbm,
    gskip_hbm,
    out_ref,
    gi_ref,
    gres_ref,
    glog_ref,
    gskip_ref,
    x_ref,
    res_ref,
    lr_ref,
    skip_ref,
    w_v,
    og,
    part,
    hall,
    x32,
    y32,
    g32,
    mb,
    rate_t,
    c_t,
    far4,
    rate8,
    a8,
    c8,
    ex8,
    in8,
    v8,
    s_own,
    s_sib,
    s_pair,
    s_recv,
    h_t,
    r_own,
    r_sib,
    r_pair,
    r_recv,
    l_t,
    red,
    rr,
    dec,
    fin,
    bx1,
    al1,
    ar1,
    al2,
    ar2,
    bl1,
    br1,
    bl2,
    br2,
    bx3,
    in_sem,
    out_sem,
    w_sem,
    ag_s,
    ag_r,
    rs_s,
    rs_r,
    sr_ss,
    s_rs,
    r_rs,
    sib_s,
    sib_r,
    p_ss,
    p_rs,
    q_ss,
    q_rs,
):
    tok, chans = x_ref.shape
    modes = res_ref.shape[0]
    dim = w_v.shape[1]
    rows = tok // (NX * NZ)
    steps = tok // SUB
    lanes = chans // LANE
    half, quarter = dim // 2, dim // 4
    a_cols = dim // PIECES
    split = A_PIECES * a_cols
    b_cols = (dim - split) // B_PIECES

    me = lax.axis_index("ctx")
    tp = lax.axis_index("tp")
    xl, z = tp // NZ, lax.rem(tp, NZ)
    ox = 1 - xl
    zr, zl, zo = lax.rem(z + 1, NZ), lax.rem(z + 3, NZ), lax.rem(z + 2, NZ)
    to_x = {"tp": ox * NZ + z}
    to_r = {"tp": xl * NZ + zr}
    to_l = {"tp": xl * NZ + zl}
    pairs = n_ctx // 2
    pair, core = me // 2, lax.rem(me, 2)
    to_sib = {"ctx": me + 1 - 2 * core}
    my_half = pl.ds(pl.multiple_of(core * (chans // 2), chans // 2), chans // 2)

    w_copy = pltpu.make_async_copy(w_hbm, w_v, w_sem)

    barrier = pltpu.get_barrier_semaphore()
    for peer in (to_x, to_r, to_l):
        pl.semaphore_signal(barrier, inc=1, device_id=peer, device_id_type=MESH)

    @pl.loop(1, n_ctx)
    def _(k):
        pl.semaphore_signal(
            barrier, inc=1, device_id={"ctx": lax.rem(me + k, n_ctx)}, device_id_type=MESH
        )

    ins = [
        pltpu.make_async_copy(src, dst, in_sem.at[i])
        for i, (src, dst) in enumerate(
            (
                (lr_hbm, lr_ref),
                (res_hbm, res_ref),
                (x_hbm, x_ref),
                (skip_hbm, skip_ref),
                (og_hbm, og.at[xl, z]),
            )
        )
    ]
    for copy in ins:
        copy.start()
    w_copy.start()

    def save(index, src, dst):
        copy = pltpu.make_async_copy(src, dst, out_sem.at[index])
        copy.start()
        return copy

    pl.semaphore_wait(barrier, n_ctx + 2)

    def ctx_copy(src, dst, send, recv, peer):
        return pltpu.make_async_remote_copy(
            src_ref=src,
            dst_ref=dst,
            send_sem=send,
            recv_sem=recv,
            device_id={"ctx": peer},
            device_id_type=MESH,
        )

    def pair_copy(src, dst, recvs, peer, sender):
        return pltpu.make_async_remote_copy(
            src_ref=src,
            dst_ref=dst.at[sender],
            send_sem=sr_ss,
            recv_sem=recvs.at[sender],
            device_id={"ctx": 2 * peer + core},
            device_id_type=MESH,
        )

    def s_copy(peer, sender):
        return pair_copy(s_pair, s_recv, s_rs, peer, sender)

    def r_copy(peer, sender):
        return pair_copy(r_pair, r_recv, r_rs, peer, sender)

    def sib_copy(index, src, dst):
        return pltpu.make_async_remote_copy(
            src_ref=src,
            dst_ref=dst,
            send_sem=sib_s.at[index],
            recv_sem=sib_r.at[index],
            device_id=to_sib,
            device_id_type=MESH,
        )

    def p_copy(peer):
        return ctx_copy(red.at[peer], rr.at[me], p_ss, p_rs, peer)

    def q_copy(peer):
        return ctx_copy(fin.at[me], fin.at[me], q_ss, q_rs, peer)

    def wait_all(ref, sem):
        rest = ref.at[pl.ds(0, n_ctx - 1)]
        pltpu.make_async_copy(rest, rest, sem).wait()

    def others(step):
        pl.loop(1, n_ctx)(lambda k: step(lax.rem(me + k, n_ctx)))

    tags = iter(range(100))

    def ag(src, dst, peer):
        index = next(tags)
        return pltpu.make_async_remote_copy(
            src_ref=src,
            dst_ref=dst,
            send_sem=ag_s,
            recv_sem=ag_r.at[index],
            device_id=peer,
            device_id_type=MESH,
        )

    def relay(shard_x, shard_z, columns, peer):
        piece = og.at[shard_x, shard_z, :, columns]
        return ag(piece, piece, peer)

    def mine(columns, peer):
        return ag(og_hbm.at[:, columns], og.at[xl, z, :, columns], peer)

    all_a, all_b = pl.ds(0, half), pl.ds(half, half)
    a1, a2 = pl.ds(0, quarter), pl.ds(quarter, quarter)
    b1, b2 = pl.ds(half, quarter), pl.ds(half + quarter, quarter)

    x_a, r_b, l_b = mine(all_a, to_x), mine(all_b, to_r), mine(all_b, to_l)
    x_b, r_a, l_a = mine(all_b, to_x), mine(all_a, to_r), mine(all_a, to_l)
    for copy in (x_a, r_b, l_b, r_a, l_a):
        copy.start()
    gathers = [x_a, r_b, l_b, r_a, l_a, x_b]

    for copy in ins[:4]:
        copy.wait()
    rate = jnp.exp(lr_ref[...]) / seq
    rate_t[...] = rate
    c_t[...] = res_ref[...] * jnp.sqrt(2.0 * rate)
    far = jnp.exp(-float(tok) * rate)
    for n in range(modes):
        row = pl.ds(n, 1)
        rate8[n] = jnp.broadcast_to(rate_t[row, :], (SUB, chans))
        c8[n] = jnp.broadcast_to(c_t[row, :], (SUB, chans))
    a8[...] = jnp.exp(-rate8[...])

    def lane(k):
        return pl.ds(k * LANE, LANE)

    for k in range(lanes):
        x32[k] = x_ref[:, lane(k)].astype(F32)
        far4[:, pl.ds(k, 1), :] = far[:, k * LANE : (k + 1) * LANE][:, None, :]

    place = lax.broadcasted_iota(jnp.int32, (modes, SUB, LANE), 1)
    place_f = place.astype(F32)
    span = float(steps)
    zero = jnp.zeros((modes, SUB, LANE), F32)

    def at_step(ref, i, k):
        return ref[k, pl.ds(i, SUB, stride=steps), :]

    for k in range(lanes):
        a = a8[:, :, lane(k)]

        def grow(i, h, a=a, k=k):
            return a * h + at_step(x32, i, k)[None]

        end = lax.fori_loop(0, steps, grow, zero, unroll=4)
        rk = rate8[:, :, lane(k)]
        for s in (1, 2, 4):
            moved = jnp.where(place >= s, pltpu.roll(end, s, 1), 0.0)
            end = end + jnp.exp(-(span * s) * rk) * moved
        ex8[:, :, lane(k)] = jnp.where(place >= 1, pltpu.roll(end, 1, 1), 0.0)
        s_own[:, lane(k)] = jnp.sum(jnp.where(place == SUB - 1, end, 0.0), axis=1)

    sib_first = sib_copy(0, s_own, s_sib)
    sib_first.start()

    far_half = jnp.exp(-float(tok) * rate_t[:, my_half])
    sib_first.wait_recv()
    mine_s, sib_s_half = s_own[:, my_half], s_sib[:, my_half]
    s_early = jnp.where(core == 0, mine_s, sib_s_half)
    s_late = jnp.where(core == 0, sib_s_half, mine_s)
    s_pair[...] = (s_late + far_half * s_early).astype(BF16)

    @pl.loop(pair + 1, pairs)
    def _(peer):
        s_copy(peer, pair).start()

    x_b.start()

    for k in range(lanes):
        a = a8[:, :, lane(k)]
        rk = rate8[:, :, lane(k)]
        for at, s in enumerate((1, 2, 4)):
            dec[at, :, :, lane(k)] = jnp.exp(-(span * s) * rk)
        dec[3, :, :, lane(k)] = jnp.exp(-span * (SUB - 1.0 - place_f) * rk)
        dec[4, :, :, lane(k)] = jnp.exp(-span * place_f * rk)

        def lift(i, carry, a=a, k=k):
            h, v = carry
            h = a * h + at_step(x32, i, k)[None]
            return h, a * v + h

        _, v = lax.fori_loop(0, steps, lift, (zero, zero), unroll=2)
        v8[:, :, lane(k)] = a * v

    r_b.wait_recv()
    l_b.wait_recv()
    r_ob, l_ob = relay(xl, zl, b1, to_r), relay(xl, zr, b2, to_l)
    x_lb, x_rb = relay(xl, zl, all_b, to_x), relay(xl, zr, all_b, to_x)
    x_a.wait_recv()
    r_xa1, l_xa2 = relay(ox, z, a1, to_r), relay(ox, z, a2, to_l)
    r_xa2, l_xa1 = relay(ox, z, a2, to_r), relay(ox, z, a1, to_l)
    for copy in (r_xa1, l_xa2, x_lb, x_rb, r_ob, l_ob, r_xa2, l_xa1):
        copy.start()
    gathers += [r_xa1, l_xa2, x_lb, x_rb, r_ob, l_ob, r_xa2, l_xa1]

    def join(sender, total):
        s_copy(0, sender).wait_recv()
        return far_half * far_half * total + s_recv[sender].astype(F32)

    none = jnp.zeros((modes, chans // 2), F32)
    h_t[:, my_half] = lax.fori_loop(0, pair, join, none)
    sib_h = sib_copy(1, h_t.at[:, my_half], h_t.at[:, my_half])
    sib_h.start()

    r_a.wait_recv()
    l_a.wait_recv()
    r_oa, l_oa = relay(xl, zl, a1, to_r), relay(xl, zr, a2, to_l)
    r_oa.start()
    l_oa.start()
    gathers += [r_oa, l_oa]

    sib_h.wait_recv()
    far = jnp.exp(-float(tok) * rate_t[...])
    h_in = jnp.where(core == 0, h_t[...], far * h_t[...] + s_sib[...])
    for n in range(modes):
        in8[n] = jnp.broadcast_to(h_in[n : n + 1], (SUB, chans))

    for k in range(lanes):
        a, c = a8[:, :, lane(k)], c8[:, :, lane(k)]
        skip = skip_ref[:, lane(k)]
        start = ex8[:, :, lane(k)] + dec[4, :, :, lane(k)] * in8[:, :, lane(k)]
        v = v8[:, :, lane(k)] + span * a * dec[0, :, :, lane(k)] * start
        v8[:, :, lane(k)] = v
        u = jnp.sum(dec[3, :, :, lane(k)] * v, axis=1, keepdims=True)
        red[:, pl.ds(2 * lanes + k, 1), :] = u

        def emit(i, h, a=a, c=c, skip=skip, k=k):
            now = at_step(x32, i, k)
            h = a * h + now[None]
            hall[i, :, :, lane(k)] = h
            y32[k, pl.ds(i, SUB, stride=steps), :] = jnp.sum(c * h, axis=0) + skip * now
            return h

        lax.fori_loop(0, steps, emit, start, unroll=2)
        mb[:, lane(k)] = y32[k].astype(BF16)

    r_xa1.wait_recv()
    l_xa2.wait_recv()
    r_oxa, l_oxa = relay(ox, zl, a1, to_r), relay(ox, zr, a2, to_l)
    r_oxa.start()
    l_oxa.start()
    gathers += [r_oxa, l_oxa]

    r_ob.wait_recv()
    x_ob1 = relay(xl, zo, b1, to_x)
    x_ob1.start()
    l_ob.wait_recv()
    x_ob2 = relay(xl, zo, b2, to_x)
    x_ob2.start()
    gathers += [x_ob1, x_ob2]
    sums = iter(range(100))
    reduces = []

    def rs(src, dst, peer):
        index = next(sums)
        copy = pltpu.make_async_remote_copy(
            src_ref=src,
            dst_ref=dst,
            send_sem=rs_s,
            recv_sem=rs_r.at[index],
            device_id=peer,
            device_id_type=MESH,
        )
        copy.start()
        reduces.append(copy)
        return copy

    def a_span(i):
        return pl.ds(i * a_cols, a_cols)

    def a_halves(i):
        h = a_cols // 2
        return pl.ds(i * a_cols, h), pl.ds(i * a_cols + h, h)

    def b_span(i):
        return pl.ds(split + i * b_cols, b_cols)

    def b_halves(i):
        h = b_cols // 2
        return pl.ds(split + i * b_cols, h), pl.ds(split + i * b_cols + h, h)

    w_copy.wait()
    for lo, hi in ((0, split), (split, dim)):
        p = jnp.dot(mb[...], w_v[:, lo:hi], preferred_element_type=F32)
        part[:, :, :, lo:hi] = p.astype(BF16).reshape(NX, NZ, rows, hi - lo)

    rs_l1, rs_r1 = [], []
    for i in range(B_PIECES):
        h1, h2 = b_halves(i)
        rs_l1.append(rs(part.at[:, zo, :, h1], bl1.at[i], to_r))
        rs_r1.append(rs(part.at[:, zo, :, h2], br1.at[i], to_l))

    rs_x1 = []

    def send_x1():
        i = len(rs_x1)
        rs_x1.append(rs(part.at[ox, :, :, a_span(i)], bx1.at[i], to_x))

    send_x1()
    send_x1()

    x_a_parts = [r_xa2, l_xa1, r_oa, l_oa, r_oxa, l_oxa]
    for copy in x_a_parts:
        copy.wait_recv()
    ins[4].wait()

    def project_back(lo, hi, fresh=False):
        left = og[:, :, :, lo:hi].reshape(tok, hi - lo)
        for k in range(lanes):
            got = lax.dot_general(
                left,
                w_v[k * LANE : (k + 1) * LANE, lo:hi],
                (((1,), (1,)), ((), ())),
                preferred_element_type=F32,
            )
            g32[k] = got if fresh else g32[k] + got

    project_back(0, half, True)

    def merge(ref, got):
        ref[...] = (ref[...].astype(F32) + got[...].astype(F32)).astype(BF16)

    rs_l2, rs_r2 = [], []

    def take_b_z1():
        i = len(rs_l2)
        h1, h2 = b_halves(i)
        rs_l1[i].wait_recv()
        merge(part.at[:, zr, :, h1], bl1.at[i])
        rs_l2.append(rs(part.at[:, zr, :, b_span(i)], bl2.at[i], to_r))
        rs_r1[i].wait_recv()
        merge(part.at[:, zl, :, h2], br1.at[i])
        rs_r2.append(rs(part.at[:, zl, :, b_span(i)], br2.at[i], to_l))

    take_b_z1()

    for copy in (x_b, x_lb, x_rb, x_ob1):
        copy.wait_recv()

    project_back(half, half + quarter)
    x_ob2.wait_recv()
    project_back(half + quarter, dim)

    for k in range(lanes):
        g32[k] = g32[k].astype(BF16).astype(F32)
        sk = jnp.sum(g32[k] * x32[k], axis=0, keepdims=True)
        red[:, pl.ds(4 * lanes + k, 1), :] = jnp.broadcast_to(sk[None], (modes, 1, LANE))

    hm = modes // 2
    zh = jnp.zeros((hm, SUB, LANE), F32)
    pm = place[:hm]
    for m0 in (0, hm):
        ms = pl.ds(m0, hm)
        for k in range(lanes):
            lv = lane(k)
            a = a8[ms, :, lv]

            def back(j, carry, a=a, k=k, lv=lv, ms=ms):
                h, gs, mloc = carry
                i = steps - 1 - j
                now = at_step(g32, i, k)[None]
                held = hall[i, ms, :, lv]
                h = a * h + now
                return h, gs + now * held, mloc + h * held

            end, gs, mloc = lax.fori_loop(0, steps, back, (zh, zh, zh), unroll=2)
            for at, s in enumerate((1, 2, 4)):
                moved = jnp.where(pm < SUB - s, pltpu.roll(end, SUB - s, 1), 0.0)
                end = end + dec[at, ms, :, lv] * moved
            ex = jnp.where(pm < SUB - 1, pltpu.roll(end, SUB - 1, 1), 0.0)
            ex8[ms, :, lv] = ex
            first = jnp.where(pm == 0, end, 0.0)
            r_own[ms, lv] = jnp.sum(first, axis=1)
            for at, value in ((0, gs), (1, mloc + ex * v8[ms, :, lv]), (3, first)):
                red[ms, pl.ds(at * lanes + k, 1), :] = jnp.sum(value, axis=1, keepdims=True)

        @pl.loop(m0, m0 + hm)
        def _(peer):
            @pl.when(peer != me)
            def _():
                p_copy(peer).start()

        if m0 == 0:
            take_b_z1()

    take_b_z1()
    sib_back = sib_copy(2, r_own, r_sib)
    sib_back.start()
    rr[me] = red[me]

    rs_al1, rs_ar1, rs_al2, rs_ar2 = [], [], [], []

    def take_x1():
        i = len(rs_al1)
        rs_x1[i].wait_recv()
        h1, h2 = a_halves(i)
        merge(part.at[xl, zo, :, a_span(i)], bx1.at[i, zo])
        rs_al1.append(rs(part.at[xl, zo, :, h1], al1.at[i], to_r))
        rs_ar1.append(rs(part.at[xl, zo, :, h2], ar1.at[i], to_l))
        merge(part.at[xl, zr, :, a_span(i)], bx1.at[i, zr])
        merge(part.at[xl, zl, :, a_span(i)], bx1.at[i, zl])

    def take_z1():
        i = len(rs_al2)
        h1, h2 = a_halves(i)
        rs_al1[i].wait_recv()
        merge(part.at[xl, zr, :, h1], al1.at[i])
        rs_al2.append(rs(part.at[xl, zr, :, a_span(i)], al2.at[i], to_r))
        rs_ar1[i].wait_recv()
        merge(part.at[xl, zl, :, h2], ar1.at[i])
        rs_ar2.append(rs(part.at[xl, zl, :, a_span(i)], ar2.at[i], to_l))

    def total3(ref, left, right):
        return ref[...].astype(F32) + left[...].astype(F32) + right[...].astype(F32)

    rs_x3 = []

    def take_b_z2():
        i = len(rs_x3)
        rs_l2[i].wait_recv()
        rs_r2[i].wait_recv()
        far_part = part.at[ox, z, :, b_span(i)]
        far_part[...] = total3(far_part, bl2.at[i, ox], br2.at[i, ox]).astype(BF16)
        rs_x3.append(rs(far_part, bx3.at[i], to_x))

    take_x1()

    sib_back.wait_recv()
    mine_r, sib_r_half = r_own[:, my_half], r_sib[:, my_half]
    r_early = jnp.where(core == 0, mine_r, sib_r_half)
    r_late = jnp.where(core == 0, sib_r_half, mine_r)
    r_pair[...] = (r_early + far_half * r_late).astype(BF16)

    @pl.loop(0, pair)
    def _(peer):
        r_copy(peer, pair).start()


    take_x1()

    take_b_z2()

    wait_all(rr, p_rs)

    far_me = far4[me]

    def owner(j, carry):
        lam, gsum, msum, ksum = carry
        sender = n_ctx - 1 - j
        got = rr[sender]
        gsum = gsum + got[:lanes]
        msum = msum + got[lanes : 2 * lanes] + lam * got[2 * lanes : 3 * lanes]
        ksum = ksum + got[4 * lanes : 5 * lanes]
        return far_me * lam + got[3 * lanes : 4 * lanes], gsum, msum, ksum

    zl4 = jnp.zeros((lanes, LANE), F32)
    _, gsum, msum, ksum = lax.fori_loop(0, n_ctx, owner, (zl4, zl4, zl4, zl4))
    fin[me, pl.ds(0, lanes), :] = gsum
    fin[me, pl.ds(lanes, lanes), :] = msum
    others(lambda peer: q_copy(peer).start())
    scale = 1.0 / math.sqrt(seq)
    gskip_ref[...] = ksum * scale
    saves = [save(0, gskip_ref, gskip_hbm)]

    take_b_z2()

    take_z1()

    take_z1()

    take_b_z2()

    def join_back(j, total):
        sender = pairs - 1 - j
        r_copy(0, sender).wait_recv()
        return far_half * far_half * total + r_recv[sender].astype(F32)

    l_t[:, my_half] = lax.fori_loop(0, pairs - 1 - pair, join_back, none)
    sib_l = sib_copy(3, l_t.at[:, my_half], l_t.at[:, my_half])
    sib_l.start()

    sib_l.wait_recv()
    l_in = jnp.where(core == 1, l_t[...], far * l_t[...] + r_sib[...])
    for n in range(modes):
        in8[n] = jnp.broadcast_to(l_in[n : n + 1], (SUB, chans))

    for k in range(lanes):
        a, c = a8[:, :, lane(k)], c8[:, :, lane(k)]
        skip = skip_ref[:, lane(k)]
        start = ex8[:, :, lane(k)] + dec[3, :, :, lane(k)] * in8[:, :, lane(k)]

        def emit_back(j, h, a=a, c=c, skip=skip, k=k):
            i = steps - 1 - j
            now = at_step(g32, i, k)
            h = a * h + now[None]
            y32[k, pl.ds(i, SUB, stride=steps), :] = jnp.sum(c * h, axis=0) + skip * now
            return h

        lax.fori_loop(0, steps, emit_back, start, unroll=2)
        gi_ref[:, lane(k)] = y32[k].astype(BF16)
    saves.append(save(1, gi_ref, gi_hbm))

    for i in range(A_PIECES):
        rs_al2[i].wait_recv()
        rs_ar2[i].wait_recv()
        out_ref[:, a_span(i)] = (
            total3(part.at[xl, z, :, a_span(i)], al2.at[i], ar2.at[i]) + bx1[i, z].astype(F32)
        ).astype(BF16)

    part_a, part_b = pl.ds(0, split), pl.ds(split, dim - split)
    saves.append(save(2, out_ref.at[:, part_a], out_hbm.at[:, part_a]))

    for i in range(B_PIECES):
        rs_x3[i].wait_recv()
        out_ref[:, b_span(i)] = (
            total3(part.at[xl, z, :, b_span(i)], bl2.at[i, xl], br2.at[i, xl])
            + bx3[i].astype(F32)
        ).astype(BF16)

    saves.append(save(3, out_ref.at[:, part_b], out_hbm.at[:, part_b]))

    wait_all(fin, q_rs)

    for k in range(lanes):
        rate = rate_t[:, lane(k)]
        gr = jnp.sum(fin[:, pl.ds(k, 1), :], axis=1)
        ml = jnp.sum(fin[:, pl.ds(lanes + k, 1), :], axis=1)
        gres_ref[:, lane(k)] = gr * (jnp.sqrt(2.0 * rate) * scale)
        glog_ref[:, lane(k)] = c_t[:, lane(k)] * ((0.5 + rate) * gr - rate * ml) * scale

    saves += [save(4, gres_ref, gres_hbm), save(5, glog_ref, glog_hbm)]

    sent = w_v.at[pl.ds(0, tok - rows)]
    pltpu.make_async_copy(sent, sent, ag_s).wait()
    pltpu.make_async_copy(sent, sent, rs_s).wait()
    for copy in (sib_first, sib_h, sib_back, sib_l):
        copy.wait_send()
    rest = s_recv.at[pl.ds(0, pairs - 1)]
    pltpu.make_async_copy(rest, rest, sr_ss).wait()
    wait_all(rr, p_ss)
    wait_all(fin, q_ss)

    for copy in saves:
        copy.wait()


def store(*refs):
    n = (len(refs) - 2) // 3
    ins, outs, bufs = refs[:n], refs[n : 2 * n], refs[2 * n : 3 * n]
    loads = [pltpu.make_async_copy(ins[i], bufs[i], refs[-2].at[i]) for i in range(n)]
    saves = [pltpu.make_async_copy(bufs[i], outs[i], refs[-1].at[i]) for i in range(n)]
    for copy in loads:
        copy.start()
    for load, copy in zip(loads, saves):
        load.wait()
        copy.start()
    for copy in saves:
        copy.wait()


def per_device(inputs, residue, log_rate, skip, out_weight, out_grad):
    n_ctx = lax.axis_size("ctx")
    tok, chans = inputs.shape
    modes = residue.shape[1]
    dim = out_weight.shape[1]
    rows = tok // (NX * NZ)
    steps = tok // SUB
    lanes = chans // LANE
    a_cols = dim // PIECES
    b_cols = (dim - A_PIECES * a_cols) // B_PIECES
    wide = (modes, SUB, chans)
    flat = (modes, chans)
    packed = -(-5 * lanes // SUB) * SUB
    anywhere = pl.BlockSpec(memory_space=pl.ANY)
    dma = pltpu.SemaphoreType.DMA
    results = (
        jax.ShapeDtypeStruct((rows, dim), BF16),
        jax.ShapeDtypeStruct((tok, chans), BF16),
        jax.ShapeDtypeStruct(flat, F32),
        jax.ShapeDtypeStruct(flat, F32),
        jax.ShapeDtypeStruct((lanes, LANE), F32),
    )
    held_shapes = [pltpu.VMEM(r.shape, r.dtype) for r in results]
    held = pl.pallas_call(
        functools.partial(kernel, tok * n_ctx, n_ctx),
        out_shape=results,
        in_specs=[anywhere] * 6,
        out_specs=(anywhere,) * 5,
        scratch_shapes=[
            *held_shapes,
            pltpu.VMEM((tok, chans), BF16),
            pltpu.VMEM(flat, F32),
            pltpu.VMEM(flat, F32),
            pltpu.VMEM((1, chans), F32),
            pltpu.VMEM((chans, dim), BF16),
            pltpu.VMEM((NX, NZ, rows, dim), BF16),
            pltpu.VMEM((NX, NZ, rows, dim), BF16),
            pltpu.VMEM((steps, *wide), F32),
            pltpu.VMEM((lanes, tok, LANE), F32),
            pltpu.VMEM((lanes, tok, LANE), F32),
            pltpu.VMEM((lanes, tok, LANE), F32),
            pltpu.VMEM((tok, chans), BF16),
            pltpu.VMEM(flat, F32),
            pltpu.VMEM(flat, F32),
            pltpu.VMEM((modes, lanes, LANE), F32),
            pltpu.VMEM(wide, F32),
            pltpu.VMEM(wide, F32),
            pltpu.VMEM(wide, F32),
            pltpu.VMEM(wide, F32),
            pltpu.VMEM(wide, F32),
            pltpu.VMEM(wide, F32),
            *[
                pltpu.VMEM(flat, F32),
                pltpu.VMEM(flat, F32),
                pltpu.VMEM((modes, chans // 2), BF16),
                pltpu.VMEM((n_ctx // 2, modes, chans // 2), BF16),
                pltpu.VMEM(flat, F32),
            ]
            * 2,
            pltpu.VMEM((modes, packed, LANE), F32),
            pltpu.VMEM((n_ctx, packed, LANE), F32),
            pltpu.VMEM((5, *wide), F32),
            pltpu.VMEM((n_ctx, 2 * lanes, LANE), F32),
            pltpu.VMEM((A_PIECES, NZ, rows, a_cols), BF16),
            pltpu.VMEM((A_PIECES, rows, a_cols // 2), BF16),
            pltpu.VMEM((A_PIECES, rows, a_cols // 2), BF16),
            pltpu.VMEM((A_PIECES, rows, a_cols), BF16),
            pltpu.VMEM((A_PIECES, rows, a_cols), BF16),
            pltpu.VMEM((B_PIECES, NX, rows, b_cols // 2), BF16),
            pltpu.VMEM((B_PIECES, NX, rows, b_cols // 2), BF16),
            pltpu.VMEM((B_PIECES, NX, rows, b_cols), BF16),
            pltpu.VMEM((B_PIECES, NX, rows, b_cols), BF16),
            pltpu.VMEM((B_PIECES, rows, b_cols), BF16),
            dma((5,)),
            dma((6,)),
            dma,
            dma,
            dma((21,)),
            dma,
            dma((5 * (A_PIECES + B_PIECES),)),
            dma,
            dma((n_ctx // 2,)),
            dma((n_ctx // 2,)),
            dma((4,)),
            dma((4,)),
            *[dma] * 4,
        ],
        compiler_params=pltpu.CompilerParams(
            collective_id=0, has_side_effects=True, vmem_limit_bytes=56 * 1024 * 1024
        ),
    )(inputs, residue.T, log_rate.T, skip.reshape(1, chans), out_weight, out_grad)
    out, gi, gres, glog, gskip = pl.pallas_call(
        store,
        out_shape=results,
        in_specs=[anywhere] * 5,
        out_specs=(anywhere,) * 5,
        scratch_shapes=[*held_shapes, dma((5,)), dma((5,))],
    )(*held)
    return out, gi, gres.T, glog.T, gskip.reshape(chans)


def solution(mesh):
    return jax.shard_map(
        per_device,
        mesh=mesh,
        in_specs=(
            P("ctx", "tp"),
            P("tp", None),
            P("tp", None),
            P("tp"),
            P("tp", None),
            P(("ctx", "tp"), None),
        ),
        out_specs=(P(("ctx", "tp"), None), P("ctx", "tp"), P("tp", None), P("tp", None), P("tp")),
        check_vma=False,
    )
```

time: 55 us -> 44.8 us (0.81)
  Pallas kernels: 54.2 us -> 44.1 us
    pallas_call x1, Pallas kernels: 52.3 us -> 42.3 us  [per_device(): pl.pallas_call(functools.partial(kernel, tok * n_ctx, n_ctx), out_shape=r...]
where the time goes in v2:
time: 44.8 us; the launch traced here: 44.7 us
  Pallas kernels  44.1 us (98%)
  between operations  0.64 us (1%)
    pallas_call x1, Pallas kernels, per_device(): pl.pallas_call(functools.partial(kernel, tok * n_ctx, n_ctx), out_shape=r...  42.3 us
    pallas_call x1, Pallas kernels, per_device(): pl.pallas_call(store, out_shape=results, in_specs=[anywhere] * 5, out_spe...  1.79 us

profile of v2, /device:TPU:1, one launch (start us, length us, event | category | flops | bytes accessed | tf_op | source)
XLA Modules:
  0.0 44.7 jit_solution(16753911079141770231)
XLA Ops:
  0.6 42.3 %shard_map.101 = (bf16[16,8192]{1,0:T(8,128)(2,1)}, bf16[128,512]{1,0:T(8,128)(2,1)}, f32[16,512]{1,0:T(8,128)}, f32[16,512]{1,0:T(8,128)}, f32[4,128]{1,0:T(4,128)}) custom-call(bf16[128,512]{1,0:T(8,128)(2,1)} %x_hbm.1, f32[16,512]{1,0:T(8,128)} %bitcast.6, f32[16,512]{1,0:T(8,128)} %bitcast.7, f32[1,512]{1,0:T(1,128)} %bitcast.8, ...), custom_call_target="tpu_custom_call" | custom-call | tf_op jit(solution)/shard_map/pallas_call | solution.py:711
  42.9 1.8 %shard_map.102 = (bf16[16,8192]{1,0:T(8,128)(2,1)}, bf16[128,512]{1,0:T(8,128)(2,1)}, f32[16,512]{1,0:T(8,128)}, f32[16,512]{1,0:T(8,128)}, f32[4,128]{1,0:T(4,128)}) custom-call(bf16[16,8192]{1,0:T(8,128)(2,1)} %get-tuple-element.15.refs_0_, bf16[128,512]{1,0:T(8,128)(2,1)} %get-tuple-element.16.refs_1_, f32[16,512]{1,0:T(8,128)} %get-tuple-element.17.refs_2_, ...), custom_call_target="tpu_custom_call" | custom-call | tf_op jit(solution)/shard_map/pallas_call | solution.py:779

commit v3 on v2

--- a/solution.py
+++ b/solution.py
@@ -14,7 +14,8 @@
 SUB = 8
 LANE = 128
 NX, NZ = 2, 4
-PIECES, A_PIECES, B_PIECES = 8, 2, 3
+PIECES, A_PIECES, B_SHARES = 8, 2, (5, 4, 3)
+B_PIECES = len(B_SHARES)
 
 
 def kernel(
@@ -59,7 +60,6 @@
     v8,
     s_own,
     s_sib,
-    s_pair,
     s_recv,
     h_t,
     r_own,
@@ -81,6 +81,7 @@
     bl2,
     br2,
     bx3,
+    near,
     in_sem,
     out_sem,
     w_sem,
@@ -88,8 +89,9 @@
     ag_r,
     rs_s,
     rs_r,
-    sr_ss,
+    s_ss,
     s_rs,
+    r_ss,
     r_rs,
     sib_s,
     sib_r,
@@ -107,7 +109,7 @@
     half, quarter = dim // 2, dim // 4
     a_cols = dim // PIECES
     split = A_PIECES * a_cols
-    b_cols = (dim - split) // B_PIECES
+    b_unit = (dim - split) // sum(B_SHARES)
 
     me = lax.axis_index("ctx")
     tp = lax.axis_index("tp")
@@ -119,20 +121,18 @@
     to_l = {"tp": xl * NZ + zl}
     pairs = n_ctx // 2
     pair, core = me // 2, lax.rem(me, 2)
-    to_sib = {"ctx": me + 1 - 2 * core}
+    y, xh, n_y = me // 4, lax.rem(pair, 2), n_ctx // 4
+    across = me + 2 - 4 * xh
+    to_sib, to_xh = {"ctx": me + 1 - 2 * core}, {"ctx": across}
+    to_x_other = {"ctx": across, "tp": ox * NZ + z}
+    to_up, to_down = {"ctx": lax.rem(me + 4, n_ctx)}, {"ctx": lax.rem(me + n_ctx - 4, n_ctx)}
     my_half = pl.ds(pl.multiple_of(core * (chans // 2), chans // 2), chans // 2)
 
     w_copy = pltpu.make_async_copy(w_hbm, w_v, w_sem)
 
     barrier = pltpu.get_barrier_semaphore()
-    for peer in (to_x, to_r, to_l):
+    for peer in (to_x, to_r, to_l, to_x_other, to_sib, to_up, to_down):
         pl.semaphore_signal(barrier, inc=1, device_id=peer, device_id_type=MESH)
-
-    @pl.loop(1, n_ctx)
-    def _(k):
-        pl.semaphore_signal(
-            barrier, inc=1, device_id={"ctx": lax.rem(me + k, n_ctx)}, device_id_type=MESH
-        )
 
     ins = [
         pltpu.make_async_copy(src, dst, in_sem.at[i])
@@ -155,7 +155,9 @@
         copy.start()
         return copy
 
-    pl.semaphore_wait(barrier, n_ctx + 2)
+    pl.semaphore_wait(barrier, 7)
+    for peer in (to_x, to_up, to_down):
+        pl.semaphore_signal(near, inc=1, device_id=peer, device_id_type=MESH)
 
     def ctx_copy(src, dst, send, recv, peer):
         return pltpu.make_async_remote_copy(
@@ -167,21 +169,15 @@
             device_id_type=MESH,
         )
 
-    def pair_copy(src, dst, recvs, peer, sender):
-        return pltpu.make_async_remote_copy(
-            src_ref=src,
-            dst_ref=dst.at[sender],
-            send_sem=sr_ss,
-            recv_sem=recvs.at[sender],
-            device_id={"ctx": 2 * peer + core},
-            device_id_type=MESH,
-        )
-
-    def s_copy(peer, sender):
-        return pair_copy(s_pair, s_recv, s_rs, peer, sender)
+    def ctx_s(src, dst, index, peer):
+        return ctx_copy(src, dst, s_ss, s_rs.at[index], peer)
+
+    def s_copy(other):
+        both = s_recv.at[pl.ds(2 * y, 2)]
+        return ctx_s(both, both, 1, 4 * other + 2 * xh + core)
 
     def r_copy(peer, sender):
-        return pair_copy(r_pair, r_recv, r_rs, peer, sender)
+        return ctx_copy(r_pair, r_recv.at[sender], r_ss.at[peer], r_rs.at[sender], 2 * peer + core)
 
     def sib_copy(index, src, dst):
         return pltpu.make_async_remote_copy(
@@ -206,35 +202,39 @@
     def others(step):
         pl.loop(1, n_ctx)(lambda k: step(lax.rem(me + k, n_ctx)))
 
-    tags = iter(range(100))
-
-    def ag(src, dst, peer):
-        index = next(tags)
-        return pltpu.make_async_remote_copy(
+    tags = iter(range(2, 100))
+
+    def ag(src, dst, peer, group):
+        copy = pltpu.make_async_remote_copy(
             src_ref=src,
             dst_ref=dst,
             send_sem=ag_s,
-            recv_sem=ag_r.at[index],
+            recv_sem=ag_r.at[next(tags) if group is None else group],
             device_id=peer,
             device_id_type=MESH,
         )
-
-    def relay(shard_x, shard_z, columns, peer):
+        copy.start()
+        return copy
+
+    def relay(shard_x, shard_z, columns, peer, group=None):
         piece = og.at[shard_x, shard_z, :, columns]
-        return ag(piece, piece, peer)
-
-    def mine(columns, peer):
-        return ag(og_hbm.at[:, columns], og.at[xl, z, :, columns], peer)
+        return ag(piece, piece, peer, group)
+
+    def mine(columns, peer, group=None):
+        return ag(og_hbm.at[:, columns], og.at[xl, z, :, columns], peer, group)
+
+    def wait_bytes(sem, depth, width):
+        size = w_v.at[pl.ds(0, depth), pl.ds(0, width)]
+        pltpu.make_async_copy(size, size, sem).wait()
 
     all_a, all_b = pl.ds(0, half), pl.ds(half, half)
     a1, a2 = pl.ds(0, quarter), pl.ds(quarter, quarter)
     b1, b2 = pl.ds(half, quarter), pl.ds(half + quarter, quarter)
-
-    x_a, r_b, l_b = mine(all_a, to_x), mine(all_b, to_r), mine(all_b, to_l)
-    x_b, r_a, l_a = mine(all_b, to_x), mine(all_a, to_r), mine(all_a, to_l)
-    for copy in (x_a, r_b, l_b, r_a, l_a):
-        copy.start()
-    gathers = [x_a, r_b, l_b, r_a, l_a, x_b]
+    late_a, late_b = 0, 1
+
+    x_a1, r_b1, l_b2 = mine(a1, to_x), mine(b1, to_r), mine(b2, to_l)
+    x_a2, r_b2, l_b1 = mine(a2, to_x), mine(b2, to_r), mine(b1, to_l)
+    r_a, l_a = mine(all_a, to_r), mine(all_a, to_l)
 
     for copy in ins[:4]:
         copy.wait()
@@ -269,7 +269,7 @@
         def grow(i, h, a=a, k=k):
             return a * h + at_step(x32, i, k)[None]
 
-        end = lax.fori_loop(0, steps, grow, zero, unroll=4)
+        end = lax.fori_loop(0, steps, grow, zero, unroll=8)
         rk = rate8[:, :, lane(k)]
         for s in (1, 2, 4):
             moved = jnp.where(place >= s, pltpu.roll(end, s, 1), 0.0)
@@ -285,13 +285,12 @@
     mine_s, sib_s_half = s_own[:, my_half], s_sib[:, my_half]
     s_early = jnp.where(core == 0, mine_s, sib_s_half)
     s_late = jnp.where(core == 0, sib_s_half, mine_s)
-    s_pair[...] = (s_late + far_half * s_early).astype(BF16)
-
-    @pl.loop(pair + 1, pairs)
-    def _(peer):
-        s_copy(peer, pair).start()
-
-    x_b.start()
+    s_recv[pair] = (s_late + far_half * s_early).astype(BF16)
+    pl.semaphore_wait(near, 3)
+    s_across = ctx_s(s_recv.at[pair], s_recv.at[pair], 0, across)
+    s_across.start()
+
+    mine(all_b, to_x, late_b)
 
     for k in range(lanes):
         a = a8[:, :, lane(k)]
@@ -306,24 +305,37 @@
             h = a * h + at_step(x32, i, k)[None]
             return h, a * v + h
 
-        _, v = lax.fori_loop(0, steps, lift, (zero, zero), unroll=2)
+        _, v = lax.fori_loop(0, steps, lift, (zero, zero), unroll=8)
         v8[:, :, lane(k)] = a * v
 
-    r_b.wait_recv()
-    l_b.wait_recv()
-    r_ob, l_ob = relay(xl, zl, b1, to_r), relay(xl, zr, b2, to_l)
-    x_lb, x_rb = relay(xl, zl, all_b, to_x), relay(xl, zr, all_b, to_x)
-    x_a.wait_recv()
-    r_xa1, l_xa2 = relay(ox, z, a1, to_r), relay(ox, z, a2, to_l)
-    r_xa2, l_xa1 = relay(ox, z, a2, to_r), relay(ox, z, a1, to_l)
-    for copy in (r_xa1, l_xa2, x_lb, x_rb, r_ob, l_ob, r_xa2, l_xa1):
-        copy.start()
-    gathers += [r_xa1, l_xa2, x_lb, x_rb, r_ob, l_ob, r_xa2, l_xa1]
+    x_a1.wait_recv()
+    r_xa1 = relay(ox, z, a1, to_r)
+    r_b1.wait_recv()
+    r_ob = relay(xl, zl, b1, to_r)
+    relay(xl, zl, b1, to_x, late_b)
+    l_b2.wait_recv()
+    l_ob = relay(xl, zr, b2, to_l)
+    relay(xl, zr, b2, to_x, late_b)
+    s_across.wait_recv()
+
+    @pl.loop(1, n_y)
+    def _(step):
+        s_copy(lax.rem(y + step, n_y)).start()
+
+    x_a2.wait_recv()
+    l_xa2 = relay(ox, z, a2, to_l)
+    r_b2.wait_recv()
+    relay(xl, zl, b2, to_x, late_b)
+    l_b1.wait_recv()
+    relay(xl, zr, b1, to_x, late_b)
+    relay(ox, z, a2, to_r, late_a)
+    relay(ox, z, a1, to_l, late_a)
 
     def join(sender, total):
-        s_copy(0, sender).wait_recv()
         return far_half * far_half * total + s_recv[sender].astype(F32)
 
+    got_y = s_recv.at[pl.ds(0, pairs - 2)]
+    pltpu.make_async_copy(got_y, got_y, s_rs.at[1]).wait()
     none = jnp.zeros((modes, chans // 2), F32)
     h_t[:, my_half] = lax.fori_loop(0, pair, join, none)
     sib_h = sib_copy(1, h_t.at[:, my_half], h_t.at[:, my_half])
@@ -331,10 +343,8 @@
 
     r_a.wait_recv()
     l_a.wait_recv()
-    r_oa, l_oa = relay(xl, zl, a1, to_r), relay(xl, zr, a2, to_l)
-    r_oa.start()
-    l_oa.start()
-    gathers += [r_oa, l_oa]
+    relay(xl, zl, a1, to_r, late_a)
+    relay(xl, zr, a2, to_l, late_a)
 
     sib_h.wait_recv()
     far = jnp.exp(-float(tok) * rate_t[...])
@@ -358,28 +368,20 @@
             y32[k, pl.ds(i, SUB, stride=steps), :] = jnp.sum(c * h, axis=0) + skip * now
             return h
 
-        lax.fori_loop(0, steps, emit, start, unroll=2)
+        lax.fori_loop(0, steps, emit, start, unroll=8)
         mb[:, lane(k)] = y32[k].astype(BF16)
 
     r_xa1.wait_recv()
     l_xa2.wait_recv()
-    r_oxa, l_oxa = relay(ox, zl, a1, to_r), relay(ox, zr, a2, to_l)
-    r_oxa.start()
-    l_oxa.start()
-    gathers += [r_oxa, l_oxa]
+    relay(ox, zl, a1, to_r, late_a)
+    relay(ox, zr, a2, to_l, late_a)
 
     r_ob.wait_recv()
-    x_ob1 = relay(xl, zo, b1, to_x)
-    x_ob1.start()
+    relay(xl, zo, b1, to_x, late_b)
     l_ob.wait_recv()
     x_ob2 = relay(xl, zo, b2, to_x)
-    x_ob2.start()
-    gathers += [x_ob1, x_ob2]
-    sums = iter(range(100))
-    reduces = []
-
-    def rs(src, dst, peer):
-        index = next(sums)
+
+    def rs(src, dst, peer, index):
         copy = pltpu.make_async_remote_copy(
             src_ref=src,
             dst_ref=dst,
@@ -389,8 +391,16 @@
             device_id_type=MESH,
         )
         copy.start()
-        reduces.append(copy)
-        return copy
+
+    at_x1, at_az1, at_az2 = 0, A_PIECES, 2 * A_PIECES
+    at_bz1 = at_az2 + 1
+    at_bz2 = at_bz1 + B_PIECES
+    at_x3 = at_bz2 + B_PIECES
+    done = {"x1": 0, "az1": 0, "bz1": 0, "bz2": 0}
+
+    def following(name):
+        done[name] += 1
+        return done[name] - 1
 
     def a_span(i):
         return pl.ds(i * a_cols, a_cols)
@@ -399,36 +409,34 @@
         h = a_cols // 2
         return pl.ds(i * a_cols, h), pl.ds(i * a_cols + h, h)
 
-    def b_span(i):
-        return pl.ds(split + i * b_cols, b_cols)
+    def b_place(i):
+        return b_unit * sum(B_SHARES[:i]), b_unit * B_SHARES[i]
+
+    def b_span(i, base=split):
+        at, width = b_place(i)
+        return pl.ds(base + at, width)
 
     def b_halves(i):
-        h = b_cols // 2
-        return pl.ds(split + i * b_cols, h), pl.ds(split + i * b_cols + h, h)
+        at, width = b_place(i)
+        return pl.ds(split + at, width // 2), pl.ds(split + at + width // 2, width // 2)
+
+    def b_half(i):
+        at, width = b_place(i)
+        return pl.ds(at // 2, width // 2)
 
     w_copy.wait()
     for lo, hi in ((0, split), (split, dim)):
         p = jnp.dot(mb[...], w_v[:, lo:hi], preferred_element_type=F32)
         part[:, :, :, lo:hi] = p.astype(BF16).reshape(NX, NZ, rows, hi - lo)
 
-    rs_l1, rs_r1 = [], []
     for i in range(B_PIECES):
         h1, h2 = b_halves(i)
-        rs_l1.append(rs(part.at[:, zo, :, h1], bl1.at[i], to_r))
-        rs_r1.append(rs(part.at[:, zo, :, h2], br1.at[i], to_l))
-
-    rs_x1 = []
-
-    def send_x1():
-        i = len(rs_x1)
-        rs_x1.append(rs(part.at[ox, :, :, a_span(i)], bx1.at[i], to_x))
-
-    send_x1()
-    send_x1()
-
-    x_a_parts = [r_xa2, l_xa1, r_oa, l_oa, r_oxa, l_oxa]
-    for copy in x_a_parts:
-        copy.wait_recv()
+        rs(part.at[:, zo, :, h1], bl1.at[:, :, b_half(i)], to_r, at_bz1 + i)
+        rs(part.at[:, zo, :, h2], br1.at[:, :, b_half(i)], to_l, at_bz1 + i)
+    for i in range(A_PIECES):
+        rs(part.at[ox, :, :, a_span(i)], bx1.at[i], to_x, at_x1 + i)
+
+    wait_bytes(ag_r.at[late_a], 6 * rows, quarter)
     ins[4].wait()
 
     def project_back(lo, hi, fresh=False):
@@ -447,22 +455,48 @@
     def merge(ref, got):
         ref[...] = (ref[...].astype(F32) + got[...].astype(F32)).astype(BF16)
 
-    rs_l2, rs_r2 = [], []
-
     def take_b_z1():
-        i = len(rs_l2)
+        i = following("bz1")
         h1, h2 = b_halves(i)
-        rs_l1[i].wait_recv()
-        merge(part.at[:, zr, :, h1], bl1.at[i])
-        rs_l2.append(rs(part.at[:, zr, :, b_span(i)], bl2.at[i], to_r))
-        rs_r1[i].wait_recv()
-        merge(part.at[:, zl, :, h2], br1.at[i])
-        rs_r2.append(rs(part.at[:, zl, :, b_span(i)], br2.at[i], to_l))
+        wait_bytes(rs_r.at[at_bz1 + i], 2 * NX * rows, b_place(i)[1] // 2)
+        merge(part.at[:, zr, :, h1], bl1.at[:, :, b_half(i)])
+        rs(part.at[:, zr, :, b_span(i)], bl2.at[:, :, b_span(i, 0)], to_r, at_bz2 + i)
+        merge(part.at[:, zl, :, h2], br1.at[:, :, b_half(i)])
+        rs(part.at[:, zl, :, b_span(i)], br2.at[:, :, b_span(i, 0)], to_l, at_bz2 + i)
+
+    def take_x1():
+        i = following("x1")
+        pltpu.make_async_copy(bx1.at[i], bx1.at[i], rs_r.at[at_x1 + i]).wait()
+        h1, h2 = a_halves(i)
+        merge(part.at[xl, zo, :, a_span(i)], bx1.at[i, zo])
+        rs(part.at[xl, zo, :, h1], al1.at[i], to_r, at_az1 + i)
+        rs(part.at[xl, zo, :, h2], ar1.at[i], to_l, at_az1 + i)
+        merge(part.at[xl, zr, :, a_span(i)], bx1.at[i, zr])
+        merge(part.at[xl, zl, :, a_span(i)], bx1.at[i, zl])
+
+    def take_z1():
+        i = following("az1")
+        h1, h2 = a_halves(i)
+        wait_bytes(rs_r.at[at_az1 + i], 2 * rows, a_cols // 2)
+        merge(part.at[xl, zr, :, h1], al1.at[i])
+        rs(part.at[xl, zr, :, a_span(i)], al2.at[i], to_r, at_az2)
+        merge(part.at[xl, zl, :, h2], ar1.at[i])
+        rs(part.at[xl, zl, :, a_span(i)], ar2.at[i], to_l, at_az2)
+
+    def total3(ref, left, right):
+        return ref[...].astype(F32) + left[...].astype(F32) + right[...].astype(F32)
+
+    def take_b_z2():
+        i = following("bz2")
+        wait_bytes(rs_r.at[at_bz2 + i], 2 * NX * rows, b_place(i)[1])
+        far_part = part.at[ox, z, :, b_span(i)]
+        here = b_span(i, 0)
+        far_part[...] = total3(far_part, bl2.at[ox, :, here], br2.at[ox, :, here]).astype(BF16)
+        rs(far_part, bx3.at[:, here], to_x, at_x3)
 
     take_b_z1()
 
-    for copy in (x_b, x_lb, x_rb, x_ob1):
-        copy.wait_recv()
+    wait_bytes(ag_r.at[late_b], 7 * rows, quarter)
 
     project_back(half, half + quarter)
     x_ob2.wait_recv()
@@ -490,7 +524,7 @@
                 h = a * h + now
                 return h, gs + now * held, mloc + h * held
 
-            end, gs, mloc = lax.fori_loop(0, steps, back, (zh, zh, zh), unroll=2)
+            end, gs, mloc = lax.fori_loop(0, steps, back, (zh, zh, zh), unroll=8)
             for at, s in enumerate((1, 2, 4)):
                 moved = jnp.where(pm < SUB - s, pltpu.roll(end, SUB - s, 1), 0.0)
                 end = end + dec[at, ms, :, lv] * moved
@@ -508,49 +542,12 @@
                 p_copy(peer).start()
 
         if m0 == 0:
+            take_x1()
             take_b_z1()
 
-    take_b_z1()
     sib_back = sib_copy(2, r_own, r_sib)
     sib_back.start()
     rr[me] = red[me]
-
-    rs_al1, rs_ar1, rs_al2, rs_ar2 = [], [], [], []
-
-    def take_x1():
-        i = len(rs_al1)
-        rs_x1[i].wait_recv()
-        h1, h2 = a_halves(i)
-        merge(part.at[xl, zo, :, a_span(i)], bx1.at[i, zo])
-        rs_al1.append(rs(part.at[xl, zo, :, h1], al1.at[i], to_r))
-        rs_ar1.append(rs(part.at[xl, zo, :, h2], ar1.at[i], to_l))
-        merge(part.at[xl, zr, :, a_span(i)], bx1.at[i, zr])
-        merge(part.at[xl, zl, :, a_span(i)], bx1.at[i, zl])
-
-    def take_z1():
-        i = len(rs_al2)
-        h1, h2 = a_halves(i)
-        rs_al1[i].wait_recv()
-        merge(part.at[xl, zr, :, h1], al1.at[i])
-        rs_al2.append(rs(part.at[xl, zr, :, a_span(i)], al2.at[i], to_r))
-        rs_ar1[i].wait_recv()
-        merge(part.at[xl, zl, :, h2], ar1.at[i])
-        rs_ar2.append(rs(part.at[xl, zl, :, a_span(i)], ar2.at[i], to_l))
-
-    def total3(ref, left, right):
-        return ref[...].astype(F32) + left[...].astype(F32) + right[...].astype(F32)
-
-    rs_x3 = []
-
-    def take_b_z2():
-        i = len(rs_x3)
-        rs_l2[i].wait_recv()
-        rs_r2[i].wait_recv()
-        far_part = part.at[ox, z, :, b_span(i)]
-        far_part[...] = total3(far_part, bl2.at[i, ox], br2.at[i, ox]).astype(BF16)
-        rs_x3.append(rs(far_part, bx3.at[i], to_x))
-
-    take_x1()
 
     sib_back.wait_recv()
     mine_r, sib_r_half = r_own[:, my_half], r_sib[:, my_half]
@@ -564,8 +561,11 @@
 
 
     take_x1()
+    take_b_z1()
 
     take_b_z2()
+
+    take_z1()
 
     wait_all(rr, p_rs)
 
@@ -593,10 +593,6 @@
 
     take_z1()
 
-    take_z1()
-
-    take_b_z2()
-
     def join_back(j, total):
         sender = pairs - 1 - j
         r_copy(0, sender).wait_recv()
@@ -605,6 +601,8 @@
     l_t[:, my_half] = lax.fori_loop(0, pairs - 1 - pair, join_back, none)
     sib_l = sib_copy(3, l_t.at[:, my_half], l_t.at[:, my_half])
     sib_l.start()
+
+    take_b_z2()
 
     sib_l.wait_recv()
     l_in = jnp.where(core == 1, l_t[...], far * l_t[...] + r_sib[...])
@@ -623,13 +621,12 @@
             y32[k, pl.ds(i, SUB, stride=steps), :] = jnp.sum(c * h, axis=0) + skip * now
             return h
 
-        lax.fori_loop(0, steps, emit_back, start, unroll=2)
+        lax.fori_loop(0, steps, emit_back, start, unroll=8)
         gi_ref[:, lane(k)] = y32[k].astype(BF16)
     saves.append(save(1, gi_ref, gi_hbm))
 
+    wait_bytes(rs_r.at[at_az2], 2 * A_PIECES * rows, a_cols)
     for i in range(A_PIECES):
-        rs_al2[i].wait_recv()
-        rs_ar2[i].wait_recv()
         out_ref[:, a_span(i)] = (
             total3(part.at[xl, z, :, a_span(i)], al2.at[i], ar2.at[i]) + bx1[i, z].astype(F32)
         ).astype(BF16)
@@ -637,12 +634,11 @@
     part_a, part_b = pl.ds(0, split), pl.ds(split, dim - split)
     saves.append(save(2, out_ref.at[:, part_a], out_hbm.at[:, part_a]))
 
-    for i in range(B_PIECES):
-        rs_x3[i].wait_recv()
-        out_ref[:, b_span(i)] = (
-            total3(part.at[xl, z, :, b_span(i)], bl2.at[i, xl], br2.at[i, xl])
-            + bx3[i].astype(F32)
-        ).astype(BF16)
+    wait_bytes(rs_r.at[at_x3], rows, dim - split)
+    out_ref[:, split:] = (
+        total3(part.at[xl, z, :, pl.ds(split, dim - split)], bl2.at[xl], br2.at[xl])
+        + bx3[...].astype(F32)
+    ).astype(BF16)
 
     saves.append(save(3, out_ref.at[:, part_b], out_hbm.at[:, part_b]))
 
@@ -662,8 +658,13 @@
     pltpu.make_async_copy(sent, sent, rs_s).wait()
     for copy in (sib_first, sib_h, sib_back, sib_l):
         copy.wait_send()
-    rest = s_recv.at[pl.ds(0, pairs - 1)]
-    pltpu.make_async_copy(rest, rest, sr_ss).wait()
+    rest = r_recv.at[pl.ds(0, pairs - 1)]
+    pltpu.make_async_copy(rest, rest, s_ss).wait()
+
+    @pl.loop(0, pair)
+    def _(peer):
+        r_copy(peer, pair).wait_send()
+
     wait_all(rr, p_ss)
     wait_all(fin, q_ss)
 
@@ -694,7 +695,7 @@
     steps = tok // SUB
     lanes = chans // LANE
     a_cols = dim // PIECES
-    b_cols = (dim - A_PIECES * a_cols) // B_PIECES
+    b_cols = dim - A_PIECES * a_cols
     wide = (modes, SUB, chans)
     flat = (modes, chans)
     packed = -(-5 * lanes // SUB) * SUB
@@ -736,14 +737,15 @@
             pltpu.VMEM(wide, F32),
             pltpu.VMEM(wide, F32),
             pltpu.VMEM(wide, F32),
-            *[
-                pltpu.VMEM(flat, F32),
-                pltpu.VMEM(flat, F32),
-                pltpu.VMEM((modes, chans // 2), BF16),
-                pltpu.VMEM((n_ctx // 2, modes, chans // 2), BF16),
-                pltpu.VMEM(flat, F32),
-            ]
-            * 2,
+            pltpu.VMEM(flat, F32),
+            pltpu.VMEM(flat, F32),
+            pltpu.VMEM((n_ctx // 2, modes, chans // 2), BF16),
+            pltpu.VMEM(flat, F32),
+            pltpu.VMEM(flat, F32),
+            pltpu.VMEM(flat, F32),
+            pltpu.VMEM((modes, chans // 2), BF16),
+            pltpu.VMEM((n_ctx // 2, modes, chans // 2), BF16),
+            pltpu.VMEM(flat, F32),
             pltpu.VMEM((modes, packed, LANE), F32),
             pltpu.VMEM((n_ctx, packed, LANE), F32),
             pltpu.VMEM((5, *wide), F32),
@@ -753,19 +755,21 @@
             pltpu.VMEM((A_PIECES, rows, a_cols // 2), BF16),
             pltpu.VMEM((A_PIECES, rows, a_cols), BF16),
             pltpu.VMEM((A_PIECES, rows, a_cols), BF16),
-            pltpu.VMEM((B_PIECES, NX, rows, b_cols // 2), BF16),
-            pltpu.VMEM((B_PIECES, NX, rows, b_cols // 2), BF16),
-            pltpu.VMEM((B_PIECES, NX, rows, b_cols), BF16),
-            pltpu.VMEM((B_PIECES, NX, rows, b_cols), BF16),
-            pltpu.VMEM((B_PIECES, rows, b_cols), BF16),
+            pltpu.VMEM((NX, rows, b_cols // 2), BF16),
+            pltpu.VMEM((NX, rows, b_cols // 2), BF16),
+            pltpu.VMEM((NX, rows, b_cols), BF16),
+            pltpu.VMEM((NX, rows, b_cols), BF16),
+            pltpu.VMEM((rows, b_cols), BF16),
+            pltpu.SemaphoreType.REGULAR,
             dma((5,)),
             dma((6,)),
             dma,
             dma,
-            dma((21,)),
+            dma((15,)),
             dma,
-            dma((5 * (A_PIECES + B_PIECES),)),
+            dma((2 * (A_PIECES + B_PIECES) + 2,)),
             dma,
+            dma((2,)),
             dma((n_ctx // 2,)),
             dma((n_ctx // 2,)),
             dma((4,)),

time: 44.8 us -> 43.3 us (0.967); the launches traced: 44.7 us -> 42.6 us
  Pallas kernels: 44.1 us -> 41.9 us
    pallas_call x1, Pallas kernels: 42.3 us -> 40.1 us  [per_device(): pl.pallas_call(functools.partial(kernel, tok * n_ctx, n_ctx), out_shape=r...]
where the time goes in v3:
time: 43.3 us; the launch traced here: 42.6 us
  Pallas kernels  41.9 us (97%)
  between operations  0.64 us (1%)
    pallas_call x1, Pallas kernels, per_device(): pl.pallas_call(functools.partial(kernel, tok * n_ctx, n_ctx), out_shape=r...  40.1 us
    pallas_call x1, Pallas kernels, per_device(): pl.pallas_call(store, out_shape=results, in_specs=[anywhere] * 5, out_spe...  1.79 us

profile of v3, /device:TPU:1, one launch (start us, length us, event | category | flops | bytes accessed | tf_op | source)
XLA Modules:
  0.0 42.6 jit_solution(9404221519567625398)
XLA Ops:
  0.6 40.1 %shard_map.101 = (bf16[16,8192]{1,0:T(8,128)(2,1)}, bf16[128,512]{1,0:T(8,128)(2,1)}, f32[16,512]{1,0:T(8,128)}, f32[16,512]{1,0:T(8,128)}, f32[4,128]{1,0:T(4,128)}) custom-call(bf16[128,512]{1,0:T(8,128)(2,1)} %x_hbm.1, f32[16,512]{1,0:T(8,128)} %bitcast.6, f32[16,512]{1,0:T(8,128)} %bitcast.7, f32[1,512]{1,0:T(1,128)} %bitcast.8, ...), custom_call_target="tpu_custom_call" | custom-call | tf_op jit(solution)/shard_map/pallas_call | solution.py:712
  40.8 1.8 %shard_map.102 = (bf16[16,8192]{1,0:T(8,128)(2,1)}, bf16[128,512]{1,0:T(8,128)(2,1)}, f32[16,512]{1,0:T(8,128)}, f32[16,512]{1,0:T(8,128)}, f32[4,128]{1,0:T(4,128)}) custom-call(bf16[16,8192]{1,0:T(8,128)(2,1)} %get-tuple-element.15.refs_0_, bf16[128,512]{1,0:T(8,128)(2,1)} %get-tuple-element.16.refs_1_, f32[16,512]{1,0:T(8,128)} %get-tuple-element.17.refs_2_, ...), custom_call_target="tpu_custom_call" | custom-call | tf_op jit(solution)/shard_map/pallas_call | solution.py:783

commit v4 on v3

--- a/solution.py
+++ b/solution.py
@@ -14,8 +14,8 @@
 SUB = 8
 LANE = 128
 NX, NZ = 2, 4
-PIECES, A_PIECES, B_SHARES = 8, 2, (5, 4, 3)
-B_PIECES = len(B_SHARES)
+SHARES, A_SHARES, B_SHARES = 32, (4, 4), (8, 8, 5, 3)
+A_PIECES, B_PIECES = len(A_SHARES), len(B_SHARES)
 
 
 def kernel(
@@ -61,7 +61,6 @@
     s_own,
     s_sib,
     s_recv,
-    h_t,
     r_own,
     r_sib,
     r_pair,
@@ -107,9 +106,8 @@
     steps = tok // SUB
     lanes = chans // LANE
     half, quarter = dim // 2, dim // 4
-    a_cols = dim // PIECES
-    split = A_PIECES * a_cols
-    b_unit = (dim - split) // sum(B_SHARES)
+    unit = dim // SHARES
+    split = unit * sum(A_SHARES)
 
     me = lax.axis_index("ctx")
     tp = lax.axis_index("tp")
@@ -282,10 +280,10 @@
 
     far_half = jnp.exp(-float(tok) * rate_t[:, my_half])
     sib_first.wait_recv()
-    mine_s, sib_s_half = s_own[:, my_half], s_sib[:, my_half]
-    s_early = jnp.where(core == 0, mine_s, sib_s_half)
-    s_late = jnp.where(core == 0, sib_s_half, mine_s)
-    s_recv[pair] = (s_late + far_half * s_early).astype(BF16)
+    s_early = jnp.where(core == 0, s_own[...], s_sib[...])
+    s_late = jnp.where(core == 0, s_sib[...], s_own[...])
+    far = jnp.exp(-float(tok) * rate_t[...])
+    s_recv[pair] = (s_late + far * s_early).astype(BF16)
     pl.semaphore_wait(near, 3)
     s_across = ctx_s(s_recv.at[pair], s_recv.at[pair], 0, across)
     s_across.start()
@@ -332,27 +330,22 @@
     relay(ox, z, a1, to_l, late_a)
 
     def join(sender, total):
-        return far_half * far_half * total + s_recv[sender].astype(F32)
+        return far * far * total + s_recv[sender].astype(F32)
 
     got_y = s_recv.at[pl.ds(0, pairs - 2)]
     pltpu.make_async_copy(got_y, got_y, s_rs.at[1]).wait()
     none = jnp.zeros((modes, chans // 2), F32)
-    h_t[:, my_half] = lax.fori_loop(0, pair, join, none)
-    sib_h = sib_copy(1, h_t.at[:, my_half], h_t.at[:, my_half])
-    sib_h.start()
+    h_in = lax.fori_loop(0, pair, join, jnp.zeros((modes, chans), F32))
+    h_in = jnp.where(core == 0, h_in, far * h_in + s_sib[...])
+    for n in range(modes):
+        in8[n] = jnp.broadcast_to(h_in[n : n + 1], (SUB, chans))
 
     r_a.wait_recv()
     l_a.wait_recv()
     relay(xl, zl, a1, to_r, late_a)
     relay(xl, zr, a2, to_l, late_a)
 
-    sib_h.wait_recv()
-    far = jnp.exp(-float(tok) * rate_t[...])
-    h_in = jnp.where(core == 0, h_t[...], far * h_t[...] + s_sib[...])
-    for n in range(modes):
-        in8[n] = jnp.broadcast_to(h_in[n : n + 1], (SUB, chans))
-
-    for k in range(lanes):
+    for k in range(lanes // 2):
         a, c = a8[:, :, lane(k)], c8[:, :, lane(k)]
         skip = skip_ref[:, lane(k)]
         start = ex8[:, :, lane(k)] + dec[4, :, :, lane(k)] * in8[:, :, lane(k)]
@@ -380,6 +373,25 @@
     relay(xl, zo, b1, to_x, late_b)
     l_ob.wait_recv()
     x_ob2 = relay(xl, zo, b2, to_x)
+
+    for k in range(lanes // 2, lanes):
+        a, c = a8[:, :, lane(k)], c8[:, :, lane(k)]
+        skip = skip_ref[:, lane(k)]
+        start = ex8[:, :, lane(k)] + dec[4, :, :, lane(k)] * in8[:, :, lane(k)]
+        v = v8[:, :, lane(k)] + span * a * dec[0, :, :, lane(k)] * start
+        v8[:, :, lane(k)] = v
+        u = jnp.sum(dec[3, :, :, lane(k)] * v, axis=1, keepdims=True)
+        red[:, pl.ds(2 * lanes + k, 1), :] = u
+
+        def emit(i, h, a=a, c=c, skip=skip, k=k):
+            now = at_step(x32, i, k)
+            h = a * h + now[None]
+            hall[i, :, :, lane(k)] = h
+            y32[k, pl.ds(i, SUB, stride=steps), :] = jnp.sum(c * h, axis=0) + skip * now
+            return h
+
+        lax.fori_loop(0, steps, emit, start, unroll=8)
+        mb[:, lane(k)] = y32[k].astype(BF16)
 
     def rs(src, dst, peer, index):
         copy = pltpu.make_async_remote_copy(
@@ -402,15 +414,22 @@
         done[name] += 1
         return done[name] - 1
 
+    def a_place(i):
+        return unit * sum(A_SHARES[:i]), unit * A_SHARES[i]
+
     def a_span(i):
-        return pl.ds(i * a_cols, a_cols)
+        return pl.ds(*a_place(i))
 
     def a_halves(i):
-        h = a_cols // 2
-        return pl.ds(i * a_cols, h), pl.ds(i * a_cols + h, h)
+        at, width = a_place(i)
+        return pl.ds(at, width // 2), pl.ds(at + width // 2, width // 2)
+
+    def a_half(i):
+        at, width = a_place(i)
+        return pl.ds(at // 2, width // 2)
 
     def b_place(i):
-        return b_unit * sum(B_SHARES[:i]), b_unit * B_SHARES[i]
+        return unit * sum(B_SHARES[:i]), unit * B_SHARES[i]
 
     def b_span(i, base=split):
         at, width = b_place(i)
@@ -425,16 +444,26 @@
         return pl.ds(at // 2, width // 2)
 
     w_copy.wait()
-    for lo, hi in ((0, split), (split, dim)):
+
+    def project(lo, hi):
         p = jnp.dot(mb[...], w_v[:, lo:hi], preferred_element_type=F32)
         part[:, :, :, lo:hi] = p.astype(BF16).reshape(NX, NZ, rows, hi - lo)
 
-    for i in range(B_PIECES):
+    def send_z1(i):
         h1, h2 = b_halves(i)
         rs(part.at[:, zo, :, h1], bl1.at[:, :, b_half(i)], to_r, at_bz1 + i)
         rs(part.at[:, zo, :, h2], br1.at[:, :, b_half(i)], to_l, at_bz1 + i)
+
+    middle = split + b_place(2)[0]
+    project(split, middle)
+    send_z1(0)
+    send_z1(1)
+    project(middle, dim)
+    for i in range(2, B_PIECES):
+        send_z1(i)
+    project(0, split)
     for i in range(A_PIECES):
-        rs(part.at[ox, :, :, a_span(i)], bx1.at[i], to_x, at_x1 + i)
+        rs(part.at[ox, :, :, a_span(i)], bx1.at[:, :, a_span(i)], to_x, at_x1 + i)
 
     wait_bytes(ag_r.at[late_a], 6 * rows, quarter)
     ins[4].wait()
@@ -466,22 +495,23 @@
 
     def take_x1():
         i = following("x1")
-        pltpu.make_async_copy(bx1.at[i], bx1.at[i], rs_r.at[at_x1 + i]).wait()
+        here = bx1.at[:, :, a_span(i)]
+        pltpu.make_async_copy(here, here, rs_r.at[at_x1 + i]).wait()
         h1, h2 = a_halves(i)
-        merge(part.at[xl, zo, :, a_span(i)], bx1.at[i, zo])
-        rs(part.at[xl, zo, :, h1], al1.at[i], to_r, at_az1 + i)
-        rs(part.at[xl, zo, :, h2], ar1.at[i], to_l, at_az1 + i)
-        merge(part.at[xl, zr, :, a_span(i)], bx1.at[i, zr])
-        merge(part.at[xl, zl, :, a_span(i)], bx1.at[i, zl])
+        merge(part.at[xl, zo, :, a_span(i)], here.at[zo])
+        rs(part.at[xl, zo, :, h1], al1.at[:, a_half(i)], to_r, at_az1 + i)
+        rs(part.at[xl, zo, :, h2], ar1.at[:, a_half(i)], to_l, at_az1 + i)
+        merge(part.at[xl, zr, :, a_span(i)], here.at[zr])
+        merge(part.at[xl, zl, :, a_span(i)], here.at[zl])
 
     def take_z1():
         i = following("az1")
         h1, h2 = a_halves(i)
-        wait_bytes(rs_r.at[at_az1 + i], 2 * rows, a_cols // 2)
-        merge(part.at[xl, zr, :, h1], al1.at[i])
-        rs(part.at[xl, zr, :, a_span(i)], al2.at[i], to_r, at_az2)
-        merge(part.at[xl, zl, :, h2], ar1.at[i])
-        rs(part.at[xl, zl, :, a_span(i)], ar2.at[i], to_l, at_az2)
+        wait_bytes(rs_r.at[at_az1 + i], 2 * rows, a_place(i)[1] // 2)
+        merge(part.at[xl, zr, :, h1], al1.at[:, a_half(i)])
+        rs(part.at[xl, zr, :, a_span(i)], al2.at[:, a_span(i)], to_r, at_az2)
+        merge(part.at[xl, zl, :, h2], ar1.at[:, a_half(i)])
+        rs(part.at[xl, zl, :, a_span(i)], ar2.at[:, a_span(i)], to_l, at_az2)
 
     def total3(ref, left, right):
         return ref[...].astype(F32) + left[...].astype(F32) + right[...].astype(F32)
@@ -494,13 +524,12 @@
         far_part[...] = total3(far_part, bl2.at[ox, :, here], br2.at[ox, :, here]).astype(BF16)
         rs(far_part, bx3.at[:, here], to_x, at_x3)
 
-    take_b_z1()
-
     wait_bytes(ag_r.at[late_b], 7 * rows, quarter)
 
     project_back(half, half + quarter)
     x_ob2.wait_recv()
     project_back(half + quarter, dim)
+    take_b_z1()
 
     for k in range(lanes):
         g32[k] = g32[k].astype(BF16).astype(F32)
@@ -562,6 +591,7 @@
 
     take_x1()
     take_b_z1()
+    take_b_z1()
 
     take_b_z2()
 
@@ -604,6 +634,8 @@
 
     take_b_z2()
 
+    take_b_z2()
+
     sib_l.wait_recv()
     l_in = jnp.where(core == 1, l_t[...], far * l_t[...] + r_sib[...])
     for n in range(modes):
@@ -625,11 +657,10 @@
         gi_ref[:, lane(k)] = y32[k].astype(BF16)
     saves.append(save(1, gi_ref, gi_hbm))
 
-    wait_bytes(rs_r.at[at_az2], 2 * A_PIECES * rows, a_cols)
-    for i in range(A_PIECES):
-        out_ref[:, a_span(i)] = (
-            total3(part.at[xl, z, :, a_span(i)], al2.at[i], ar2.at[i]) + bx1[i, z].astype(F32)
-        ).astype(BF16)
+    wait_bytes(rs_r.at[at_az2], 2 * rows, split)
+    out_ref[:, :split] = (
+        total3(part.at[xl, z, :, pl.ds(0, split)], al2, ar2) + bx1[z].astype(F32)
+    ).astype(BF16)
 
     part_a, part_b = pl.ds(0, split), pl.ds(split, dim - split)
     saves.append(save(2, out_ref.at[:, part_a], out_hbm.at[:, part_a]))
@@ -656,9 +687,9 @@
     sent = w_v.at[pl.ds(0, tok - rows)]
     pltpu.make_async_copy(sent, sent, ag_s).wait()
     pltpu.make_async_copy(sent, sent, rs_s).wait()
-    for copy in (sib_first, sib_h, sib_back, sib_l):
+    for copy in (sib_first, sib_back, sib_l):
         copy.wait_send()
-    rest = r_recv.at[pl.ds(0, pairs - 1)]
+    rest = s_recv.at[pl.ds(0, 2 * n_y - 1)]
     pltpu.make_async_copy(rest, rest, s_ss).wait()
 
     @pl.loop(0, pair)
@@ -694,8 +725,8 @@
     rows = tok // (NX * NZ)
     steps = tok // SUB
     lanes = chans // LANE
-    a_cols = dim // PIECES
-    b_cols = dim - A_PIECES * a_cols
+    split = dim // SHARES * sum(A_SHARES)
+    b_cols = dim - split
     wide = (modes, SUB, chans)
     flat = (modes, chans)
     packed = -(-5 * lanes // SUB) * SUB
@@ -739,8 +770,7 @@
             pltpu.VMEM(wide, F32),
             pltpu.VMEM(flat, F32),
             pltpu.VMEM(flat, F32),
-            pltpu.VMEM((n_ctx // 2, modes, chans // 2), BF16),
-            pltpu.VMEM(flat, F32),
+            pltpu.VMEM((n_ctx // 2, modes, chans), BF16),
             pltpu.VMEM(flat, F32),
             pltpu.VMEM(flat, F32),
             pltpu.VMEM((modes, chans // 2), BF16),
@@ -750,11 +780,11 @@
             pltpu.VMEM((n_ctx, packed, LANE), F32),
             pltpu.VMEM((5, *wide), F32),
             pltpu.VMEM((n_ctx, 2 * lanes, LANE), F32),
-            pltpu.VMEM((A_PIECES, NZ, rows, a_cols), BF16),
-            pltpu.VMEM((A_PIECES, rows, a_cols // 2), BF16),
-            pltpu.VMEM((A_PIECES, rows, a_cols // 2), BF16),
-            pltpu.VMEM((A_PIECES, rows, a_cols), BF16),
-            pltpu.VMEM((A_PIECES, rows, a_cols), BF16),
+            pltpu.VMEM((NZ, rows, split), BF16),
+            pltpu.VMEM((rows, split // 2), BF16),
+            pltpu.VMEM((rows, split // 2), BF16),
+            pltpu.VMEM((rows, split), BF16),
+            pltpu.VMEM((rows, split), BF16),
             pltpu.VMEM((NX, rows, b_cols // 2), BF16),
             pltpu.VMEM((NX, rows, b_cols // 2), BF16),
             pltpu.VMEM((NX, rows, b_cols), BF16),

time: 43.3 us -> 41.8 us (0.965)
  Pallas kernels: 41.9 us -> 40.6 us
    pallas_call x1, Pallas kernels: 40.1 us -> 38.8 us  [per_device(): pl.pallas_call(functools.partial(kernel, tok * n_ctx, n_ctx), out_shape=r...]
where the time goes in v4:
time: 41.8 us; the launch traced here: 41.2 us
  Pallas kernels  40.6 us (97%)
  between operations  0.64 us (2%)
    pallas_call x1, Pallas kernels, per_device(): pl.pallas_call(functools.partial(kernel, tok * n_ctx, n_ctx), out_shape=r...  38.8 us
    pallas_call x1, Pallas kernels, per_device(): pl.pallas_call(store, out_shape=results, in_specs=[anywhere] * 5, out_spe...  1.79 us

profile of v4, /device:TPU:1, one launch (start us, length us, event | category | flops | bytes accessed | tf_op | source)
XLA Modules:
  0.0 41.2 jit_solution(13362289702254860647)
XLA Ops:
  0.6 38.8 %shard_map.101 = (bf16[16,8192]{1,0:T(8,128)(2,1)}, bf16[128,512]{1,0:T(8,128)(2,1)}, f32[16,512]{1,0:T(8,128)}, f32[16,512]{1,0:T(8,128)}, f32[4,128]{1,0:T(4,128)}) custom-call(bf16[128,512]{1,0:T(8,128)(2,1)} %x_hbm.1, f32[16,512]{1,0:T(8,128)} %bitcast.6, f32[16,512]{1,0:T(8,128)} %bitcast.7, f32[1,512]{1,0:T(1,128)} %bitcast.8, ...), custom_call_target="tpu_custom_call" | custom-call | tf_op jit(solution)/shard_map/pallas_call | solution.py:743
  39.4 1.8 %shard_map.102 = (bf16[16,8192]{1,0:T(8,128)(2,1)}, bf16[128,512]{1,0:T(8,128)(2,1)}, f32[16,512]{1,0:T(8,128)}, f32[16,512]{1,0:T(8,128)}, f32[4,128]{1,0:T(4,128)}) custom-call(bf16[16,8192]{1,0:T(8,128)(2,1)} %get-tuple-element.15.refs_0_, bf16[128,512]{1,0:T(8,128)(2,1)} %get-tuple-element.16.refs_1_, f32[16,512]{1,0:T(8,128)} %get-tuple-element.17.refs_2_, ...), custom_call_target="tpu_custom_call" | custom-call | tf_op jit(solution)/shard_map/pallas_call | solution.py:813

commit v5 on v4

--- a/solution.py
+++ b/solution.py
@@ -27,11 +27,6 @@
     skip_hbm,
     w_hbm,
     og_hbm,
-    out_hbm,
-    gi_hbm,
-    gres_hbm,
-    glog_hbm,
-    gskip_hbm,
     out_ref,
     gi_ref,
     gres_ref,
@@ -82,7 +77,6 @@
     bx3,
     near,
     in_sem,
-    out_sem,
     w_sem,
     ag_s,
     ag_r,
@@ -148,11 +142,6 @@
         copy.start()
     w_copy.start()
 
-    def save(index, src, dst):
-        copy = pltpu.make_async_copy(src, dst, out_sem.at[index])
-        copy.start()
-        return copy
-
     pl.semaphore_wait(barrier, 7)
     for peer in (to_x, to_up, to_down):
         pl.semaphore_signal(near, inc=1, device_id=peer, device_id_type=MESH)
@@ -232,7 +221,6 @@
 
     x_a1, r_b1, l_b2 = mine(a1, to_x), mine(b1, to_r), mine(b2, to_l)
     x_a2, r_b2, l_b1 = mine(a2, to_x), mine(b2, to_r), mine(b1, to_l)
-    r_a, l_a = mine(all_a, to_r), mine(all_a, to_l)
 
     for copy in ins[:4]:
         copy.wait()
@@ -278,6 +266,8 @@
     sib_first = sib_copy(0, s_own, s_sib)
     sib_first.start()
 
+    r_a, l_a = mine(all_a, to_r), mine(all_a, to_l)
+
     far_half = jnp.exp(-float(tok) * rate_t[:, my_half])
     sib_first.wait_recv()
     s_early = jnp.where(core == 0, s_own[...], s_sib[...])
@@ -524,12 +514,13 @@
         far_part[...] = total3(far_part, bl2.at[ox, :, here], br2.at[ox, :, here]).astype(BF16)
         rs(far_part, bx3.at[:, here], to_x, at_x3)
 
+    take_b_z1()
+
     wait_bytes(ag_r.at[late_b], 7 * rows, quarter)
 
     project_back(half, half + quarter)
     x_ob2.wait_recv()
     project_back(half + quarter, dim)
-    take_b_z1()
 
     for k in range(lanes):
         g32[k] = g32[k].astype(BF16).astype(F32)
@@ -617,7 +608,6 @@
     others(lambda peer: q_copy(peer).start())
     scale = 1.0 / math.sqrt(seq)
     gskip_ref[...] = ksum * scale
-    saves = [save(0, gskip_ref, gskip_hbm)]
 
     take_b_z2()
 
@@ -655,15 +645,11 @@
 
         lax.fori_loop(0, steps, emit_back, start, unroll=8)
         gi_ref[:, lane(k)] = y32[k].astype(BF16)
-    saves.append(save(1, gi_ref, gi_hbm))
 
     wait_bytes(rs_r.at[at_az2], 2 * rows, split)
     out_ref[:, :split] = (
         total3(part.at[xl, z, :, pl.ds(0, split)], al2, ar2) + bx1[z].astype(F32)
     ).astype(BF16)
-
-    part_a, part_b = pl.ds(0, split), pl.ds(split, dim - split)
-    saves.append(save(2, out_ref.at[:, part_a], out_hbm.at[:, part_a]))
 
     wait_bytes(rs_r.at[at_x3], rows, dim - split)
     out_ref[:, split:] = (
@@ -671,7 +657,6 @@
         + bx3[...].astype(F32)
     ).astype(BF16)
 
-    saves.append(save(3, out_ref.at[:, part_b], out_hbm.at[:, part_b]))
 
     wait_all(fin, q_rs)
 
@@ -682,7 +667,6 @@
         gres_ref[:, lane(k)] = gr * (jnp.sqrt(2.0 * rate) * scale)
         glog_ref[:, lane(k)] = c_t[:, lane(k)] * ((0.5 + rate) * gr - rate * ml) * scale
 
-    saves += [save(4, gres_ref, gres_hbm), save(5, glog_ref, glog_hbm)]
 
     sent = w_v.at[pl.ds(0, tok - rows)]
     pltpu.make_async_copy(sent, sent, ag_s).wait()
@@ -699,21 +683,13 @@
     wait_all(rr, p_ss)
     wait_all(fin, q_ss)
 
-    for copy in saves:
-        copy.wait()
-
 
 def store(*refs):
-    n = (len(refs) - 2) // 3
-    ins, outs, bufs = refs[:n], refs[n : 2 * n], refs[2 * n : 3 * n]
-    loads = [pltpu.make_async_copy(ins[i], bufs[i], refs[-2].at[i]) for i in range(n)]
-    saves = [pltpu.make_async_copy(bufs[i], outs[i], refs[-1].at[i]) for i in range(n)]
-    for copy in loads:
+    n = len(refs) // 2
+    copies = [pltpu.make_async_copy(refs[i], refs[n + i], refs[-1].at[i]) for i in range(n)]
+    for copy in copies:
         copy.start()
-    for load, copy in zip(loads, saves):
-        load.wait()
-        copy.start()
-    for copy in saves:
+    for copy in copies:
         copy.wait()
 
 
@@ -739,14 +715,13 @@
         jax.ShapeDtypeStruct(flat, F32),
         jax.ShapeDtypeStruct((lanes, LANE), F32),
     )
-    held_shapes = [pltpu.VMEM(r.shape, r.dtype) for r in results]
+    vmem = pl.BlockSpec(memory_space=pltpu.VMEM)
     held = pl.pallas_call(
         functools.partial(kernel, tok * n_ctx, n_ctx),
-        out_shape=results,
+        out_shape=tuple(pltpu.VMEM(r.shape, r.dtype) for r in results),
         in_specs=[anywhere] * 6,
-        out_specs=(anywhere,) * 5,
+        out_specs=(vmem,) * 5,
         scratch_shapes=[
-            *held_shapes,
             pltpu.VMEM((tok, chans), BF16),
             pltpu.VMEM(flat, F32),
             pltpu.VMEM(flat, F32),
@@ -792,7 +767,6 @@
             pltpu.VMEM((rows, b_cols), BF16),
             pltpu.SemaphoreType.REGULAR,
             dma((5,)),
-            dma((6,)),
             dma,
             dma,
             dma((15,)),
@@ -813,9 +787,10 @@
     out, gi, gres, glog, gskip = pl.pallas_call(
         store,
         out_shape=results,
-        in_specs=[anywhere] * 5,
+        in_specs=[vmem] * 5,
         out_specs=(anywhere,) * 5,
-        scratch_shapes=[*held_shapes, dma((5,)), dma((5,))],
+        scratch_shapes=[dma((5,))],
+        compiler_params=pltpu.CompilerParams(vmem_limit_bytes=2 * 1024 * 1024),
     )(*held)
     return out, gi, gres.T, glog.T, gskip.reshape(chans)
 

time: 41.8 us -> 40 us (0.957); the launches traced: 41.2 us -> 39.9 us
  Pallas kernels: 40.6 us -> 39.2 us
    pallas_call x2, Pallas kernels: 40.6 us -> 39.2 us  [the longest x1 38.4 us: per_device(): pl.pallas_call(functools.partial(kernel, tok * n_ctx, n_ctx), out_shape=t...]
where the time goes in v5:
time: 40 us; the launch traced here: 39.9 us
  Pallas kernels  39.2 us (98%)
  between operations  0.64 us (2%)
    pallas_call x1, Pallas kernels, per_device(): pl.pallas_call(functools.partial(kernel, tok * n_ctx, n_ctx), out_shape=t...  38.4 us
    pallas_call x1, Pallas kernels, per_device(): pl.pallas_call(store, out_shape=results, in_specs=[vmem] * 5, out_specs=(...  0.8 us

profile of v5, /device:TPU:1, one launch (start us, length us, event | category | flops | bytes accessed | tf_op | source)
XLA Modules:
  0.0 39.9 jit_solution(14462996101762167904)
XLA Ops:
  0.6 38.4 %shard_map.101 = (bf16[16,8192]{1,0:T(8,128)(2,1)S(1)}, bf16[128,512]{1,0:T(8,128)(2,1)S(1)}, f32[16,512]{1,0:T(8,128)S(1)}, f32[16,512]{1,0:T(8,128)S(1)}, f32[4,128]{1,0:T(4,128)S(1)}) custom-call(bf16[128,512]{1,0:T(8,128)(2,1)} %x_hbm.1, f32[16,512]{1,0:T(8,128)} %bitcast.6, f32[16,512]{1,0:T(8,128)} %bitcast.7, f32[1,512]{1,0:T(1,128)} %bitcast.8, ...), custom_call_target="tpu_custom_call" | custom-call | tf_op jit(solution)/shard_map/pallas_call | solution.py:719
  39.1 0.8 %shard_map.102 = (bf16[16,8192]{1,0:T(8,128)(2,1)}, bf16[128,512]{1,0:T(8,128)(2,1)}, f32[16,512]{1,0:T(8,128)}, f32[16,512]{1,0:T(8,128)}, f32[4,128]{1,0:T(4,128)}) custom-call(bf16[16,8192]{1,0:T(8,128)(2,1)S(1)} %get-tuple-element.15.refs_0_, bf16[128,512]{1,0:T(8,128)(2,1)S(1)} %get-tuple-element.16.refs_1_, f32[16,512]{1,0:T(8,128)S(1)} %get-tuple-element.17.refs_2_, ...), custom_call_target="tpu_custom_call" | custom-call | tf_op jit(solution)/shard_map/pallas_call | solution.py:787

commit v6 on v5

--- a/solution.py
+++ b/solution.py
@@ -170,14 +170,15 @@
         return pltpu.make_async_remote_copy(
             src_ref=src,
             dst_ref=dst,
-            send_sem=sib_s.at[index],
+            send_sem=sib_s,
             recv_sem=sib_r.at[index],
             device_id=to_sib,
             device_id_type=MESH,
         )
 
     def p_copy(peer):
-        return ctx_copy(red.at[peer], rr.at[me], p_ss, p_rs, peer)
+        used = pl.ds(0, 5 * lanes)
+        return ctx_copy(red.at[peer, used], rr.at[me, used], p_ss, p_rs, peer)
 
     def q_copy(peer):
         return ctx_copy(fin.at[me], fin.at[me], q_ss, q_rs, peer)
@@ -255,7 +256,7 @@
         def grow(i, h, a=a, k=k):
             return a * h + at_step(x32, i, k)[None]
 
-        end = lax.fori_loop(0, steps, grow, zero, unroll=8)
+        end = lax.fori_loop(0, steps, grow, zero, unroll=16)
         rk = rate8[:, :, lane(k)]
         for s in (1, 2, 4):
             moved = jnp.where(place >= s, pltpu.roll(end, s, 1), 0.0)
@@ -293,7 +294,7 @@
             h = a * h + at_step(x32, i, k)[None]
             return h, a * v + h
 
-        _, v = lax.fori_loop(0, steps, lift, (zero, zero), unroll=8)
+        _, v = lax.fori_loop(0, steps, lift, (zero, zero), unroll=16)
         v8[:, :, lane(k)] = a * v
 
     x_a1.wait_recv()
@@ -351,7 +352,7 @@
             y32[k, pl.ds(i, SUB, stride=steps), :] = jnp.sum(c * h, axis=0) + skip * now
             return h
 
-        lax.fori_loop(0, steps, emit, start, unroll=8)
+        lax.fori_loop(0, steps, emit, start, unroll=16)
         mb[:, lane(k)] = y32[k].astype(BF16)
 
     r_xa1.wait_recv()
@@ -380,7 +381,7 @@
             y32[k, pl.ds(i, SUB, stride=steps), :] = jnp.sum(c * h, axis=0) + skip * now
             return h
 
-        lax.fori_loop(0, steps, emit, start, unroll=8)
+        lax.fori_loop(0, steps, emit, start, unroll=16)
         mb[:, lane(k)] = y32[k].astype(BF16)
 
     def rs(src, dst, peer, index):
@@ -544,7 +545,7 @@
                 h = a * h + now
                 return h, gs + now * held, mloc + h * held
 
-            end, gs, mloc = lax.fori_loop(0, steps, back, (zh, zh, zh), unroll=8)
+            end, gs, mloc = lax.fori_loop(0, steps, back, (zh, zh, zh), unroll=16)
             for at, s in enumerate((1, 2, 4)):
                 moved = jnp.where(pm < SUB - s, pltpu.roll(end, SUB - s, 1), 0.0)
                 end = end + dec[at, ms, :, lv] * moved
@@ -588,7 +589,7 @@
 
     take_z1()
 
-    wait_all(rr, p_rs)
+    wait_all(rr.at[:, pl.ds(0, 5 * lanes)], p_rs)
 
     far_me = far4[me]
 
@@ -643,7 +644,7 @@
             y32[k, pl.ds(i, SUB, stride=steps), :] = jnp.sum(c * h, axis=0) + skip * now
             return h
 
-        lax.fori_loop(0, steps, emit_back, start, unroll=8)
+        lax.fori_loop(0, steps, emit_back, start, unroll=16)
         gi_ref[:, lane(k)] = y32[k].astype(BF16)
 
     wait_bytes(rs_r.at[at_az2], 2 * rows, split)
@@ -671,8 +672,7 @@
     sent = w_v.at[pl.ds(0, tok - rows)]
     pltpu.make_async_copy(sent, sent, ag_s).wait()
     pltpu.make_async_copy(sent, sent, rs_s).wait()
-    for copy in (sib_first, sib_back, sib_l):
-        copy.wait_send()
+    wait_bytes(sib_s, rows, 5 * chans)
     rest = s_recv.at[pl.ds(0, 2 * n_y - 1)]
     pltpu.make_async_copy(rest, rest, s_ss).wait()
 
@@ -680,7 +680,7 @@
     def _(peer):
         r_copy(peer, pair).wait_send()
 
-    wait_all(rr, p_ss)
+    wait_all(rr.at[:, pl.ds(0, 5 * lanes)], p_ss)
     wait_all(fin, q_ss)
 
 
@@ -776,7 +776,7 @@
             dma((2,)),
             dma((n_ctx // 2,)),
             dma((n_ctx // 2,)),
-            dma((4,)),
+            dma,
             dma((4,)),
             *[dma] * 4,
         ],

time: 40 us -> 40.1 us (level); the launches traced: 39.9 us -> 39.4 us
  Pallas kernels: 39.2 us -> 38.7 us
    pallas_call x1, Pallas kernels: 38.4 us -> 37.9 us  [per_device(): pl.pallas_call(functools.partial(kernel, tok * n_ctx, n_ctx), out_shape=t...]
where the time goes in v6:
time: 40.1 us; the launch traced here: 39.4 us
  Pallas kernels  38.7 us (97%)
  between operations  0.64 us (2%)
    pallas_call x1, Pallas kernels, per_device(): pl.pallas_call(functools.partial(kernel, tok * n_ctx, n_ctx), out_shape=t...  37.9 us
    pallas_call x1, Pallas kernels, per_device(): pl.pallas_call(store, out_shape=results, in_specs=[vmem] * 5, out_specs=(...  0.8 us

profile of v6, /device:TPU:1, one launch (start us, length us, event | category | flops | bytes accessed | tf_op | source)
XLA Modules:
  0.0 39.4 jit_solution(9142759910756451744)
XLA Ops:
  0.6 37.9 %shard_map.101 = (bf16[16,8192]{1,0:T(8,128)(2,1)S(1)}, bf16[128,512]{1,0:T(8,128)(2,1)S(1)}, f32[16,512]{1,0:T(8,128)S(1)}, f32[16,512]{1,0:T(8,128)S(1)}, f32[4,128]{1,0:T(4,128)S(1)}) custom-call(bf16[128,512]{1,0:T(8,128)(2,1)} %x_hbm.1, f32[16,512]{1,0:T(8,128)} %bitcast.6, f32[16,512]{1,0:T(8,128)} %bitcast.7, f32[1,512]{1,0:T(1,128)} %bitcast.8, ...), custom_call_target="tpu_custom_call" | custom-call | tf_op jit(solution)/shard_map/pallas_call | solution.py:719
  38.6 0.8 %shard_map.102 = (bf16[16,8192]{1,0:T(8,128)(2,1)}, bf16[128,512]{1,0:T(8,128)(2,1)}, f32[16,512]{1,0:T(8,128)}, f32[16,512]{1,0:T(8,128)}, f32[4,128]{1,0:T(4,128)}) custom-call(bf16[16,8192]{1,0:T(8,128)(2,1)S(1)} %get-tuple-element.15.refs_0_, bf16[128,512]{1,0:T(8,128)(2,1)S(1)} %get-tuple-element.16.refs_1_, f32[16,512]{1,0:T(8,128)S(1)} %get-tuple-element.17.refs_2_, ...), custom_call_target="tpu_custom_call" | custom-call | tf_op jit(solution)/shard_map/pallas_call | solution.py:787

commit v7 on v6

--- a/solution.py
+++ b/solution.py
@@ -14,7 +14,7 @@
 SUB = 8
 LANE = 128
 NX, NZ = 2, 4
-SHARES, A_SHARES, B_SHARES = 32, (4, 4), (8, 8, 5, 3)
+SHARES, A_SHARES, B_SHARES = 32, (4, 4), (9, 8, 5, 2)
 A_PIECES, B_PIECES = len(A_SHARES), len(B_SHARES)
 
 

time: 40.1 us -> 40.1 us (level)
  no operation moved by 1% of the time
where the time goes in v7:
time: 40.1 us; the launch traced here: 39.5 us
  Pallas kernels  38.8 us (97%)
  between operations  0.64 us (2%)
    pallas_call x1, Pallas kernels, per_device(): pl.pallas_call(functools.partial(kernel, tok * n_ctx, n_ctx), out_shape=t...  38 us
    pallas_call x1, Pallas kernels, per_device(): pl.pallas_call(store, out_shape=results, in_specs=[vmem] * 5, out_specs=(...  0.8 us

profile of v7, /device:TPU:1, one launch (start us, length us, event | category | flops | bytes accessed | tf_op | source)
XLA Modules:
  0.0 39.5 jit_solution(11461023004986046898)
XLA Ops:
  0.6 38.0 %shard_map.101 = (bf16[16,8192]{1,0:T(8,128)(2,1)S(1)}, bf16[128,512]{1,0:T(8,128)(2,1)S(1)}, f32[16,512]{1,0:T(8,128)S(1)}, f32[16,512]{1,0:T(8,128)S(1)}, f32[4,128]{1,0:T(4,128)S(1)}) custom-call(bf16[128,512]{1,0:T(8,128)(2,1)} %x_hbm.1, f32[16,512]{1,0:T(8,128)} %bitcast.6, f32[16,512]{1,0:T(8,128)} %bitcast.7, f32[1,512]{1,0:T(1,128)} %bitcast.8, ...), custom_call_target="tpu_custom_call" | custom-call | tf_op jit(solution)/shard_map/pallas_call | solution.py:719
  38.7 0.8 %shard_map.102 = (bf16[16,8192]{1,0:T(8,128)(2,1)}, bf16[128,512]{1,0:T(8,128)(2,1)}, f32[16,512]{1,0:T(8,128)}, f32[16,512]{1,0:T(8,128)}, f32[4,128]{1,0:T(4,128)}) custom-call(bf16[16,8192]{1,0:T(8,128)(2,1)S(1)} %get-tuple-element.15.refs_0_, bf16[128,512]{1,0:T(8,128)(2,1)S(1)} %get-tuple-element.16.refs_1_, f32[16,512]{1,0:T(8,128)S(1)} %get-tuple-element.17.refs_2_, ...), custom_call_target="tpu_custom_call" | custom-call | tf_op jit(solution)/shard_map/pallas_call | solution.py:787
